TPU v7x, 32 devices: a whole 2x2x4 slice. The times are simulated.
32 devices in a mesh: groups: 2 (over y), wide: 8 (over z, x), narrow: 2 (over core).
Axes of the slice: x: 2, y: 2, z: 4, core: 2. Of those that a mesh axis runs over, the one named last changes fastest.
Arguments:
- queries: bfloat16 [16384, 1024], P(('groups', 'wide', 'narrow')), parts along dimension 0, may hold values from -6 to 6
- latents: bfloat16 [256, 1024], P(('groups', 'wide', 'narrow')), parts along dimension 0
- norm_gains: float32 [2, 1024], replicated, may hold values from 0.5 to 1.5
- q_weight: bfloat16 [2, 1024, 1024], P(None, 'narrow'), may hold values from -0.1875 to 0.1875
- k_weight: bfloat16 [2, 1024, 1024], P(None, 'narrow'), may hold values from -0.1875 to 0.1875
- v_weight: bfloat16 [2, 1024, 1024], P(None, 'narrow'), may hold values from -0.1875 to 0.1875
- o_weight: bfloat16 [2, 1024, 1024], P(None, 'narrow'), may hold values from -0.1875 to 0.1875
Outputs:
- decoded: bfloat16 [16384, 1024], P(('groups', 'wide', 'narrow')), parts along dimension 0
There are 2 independent parts, one for each index of `groups`. A program takes and returns all parts, laid end to end along the dimension named above; an argument that names none is the same for every part. Nothing has to cross between parts.
All inputs are finite; a program needn't handle non-finite values.
Results may differ from a plain program's by a relative error of at most 0.025.
The roundings to bfloat16 on the way count: a program that leaves them out, or rounds other values in their place, can miss the bound.
Values may be sent and summed in bfloat16 or wider, within the bound.
No kernel may reach another device: no remote copies, remote signals or barrier semaphores. Data moves between devices by JAX's collectives and lax.ppermute only.
A program may use at most 128 MiB of HBM per device.

v0:
```python
import math

import jax
import jax.numpy as jnp
from jax import lax
from jax.sharding import PartitionSpec as P

HEADS = 16
LAYERS = 2


def layer_norm(row_data, gain):
    values = row_data.astype(jnp.float32)
    center = values - jnp.mean(values, axis=-1, keepdims=True)
    spread = jnp.mean(center * center, axis=-1, keepdims=True)
    return (center * lax.rsqrt(spread + 1e-05) * gain).astype(jnp.bfloat16)


def accumulate(left_rows, panel_piece):
    return jnp.dot(left_rows, panel_piece, preferred_element_type=jnp.float32)


def project_queries(normed, panel):
    initial = jnp.zeros((normed.shape[0], panel.shape[1]), jnp.float32)

    def add_panel(running, panel_piece, row_start):
        return accumulate(normed, panel_piece)

    return add_panel(initial, lax.all_gather(panel, "narrow", axis=0, tiled=True), jnp.int32(0))


def project_output(attended, panel):
    initial = jnp.zeros((attended.shape[0], panel.shape[1]), jnp.float32)

    def add_panel(running, panel_piece, row_start):
        return accumulate(attended, panel_piece)

    return add_panel(initial, lax.all_gather(panel, "narrow", axis=0, tiled=True), jnp.int32(0))


def project_latents(source, key_panel, value_panel):
    key_sums = accumulate(source, lax.all_gather(key_panel, "narrow", axis=0, tiled=True))
    value_sums = accumulate(source, lax.all_gather(value_panel, "narrow", axis=0, tiled=True))
    return (key_sums.astype(jnp.bfloat16), value_sums.astype(jnp.bfloat16))


def attend_rows(carried, pieces, query_heads):
    key_rows, value_rows = pieces
    key_count = key_rows.shape[0]
    head_count = query_heads.shape[1]
    head_size = query_heads.shape[2]
    block_rows = math.gcd(key_count, 256)
    key_blocks = key_rows.reshape(key_count // block_rows, block_rows, head_count, head_size)
    value_blocks = value_rows.reshape(key_count // block_rows, block_rows, head_count, head_size)

    def fold_step(current, blocks_now):
        row_max, row_sum, weighted = current
        key_block, value_block = blocks_now
        scores = jnp.einsum(
            "qhd,khd->hqk", query_heads, key_block, preferred_element_type=jnp.float32
        )
        new_max = jnp.maximum(row_max, jnp.max(scores, axis=-1))
        rescale = jnp.exp(row_max - new_max)
        expo = jnp.exp(scores - new_max[:, :, None])
        row_sum = row_sum * rescale + jnp.sum(expo, axis=-1)
        mixed_sum = jnp.einsum(
            "hqk,khd->qhd",
            expo.astype(jnp.bfloat16),
            value_block,
            preferred_element_type=jnp.float32,
        )
        weighted = weighted * jnp.transpose(rescale)[:, :, None] + mixed_sum
        return ((new_max, row_sum, weighted), None)

    carried, unused = lax.scan(fold_step, carried, (key_blocks, value_blocks))
    return carried


def shards(queries, latents, norm_gains, q_weight, k_weight, v_weight, o_weight):
    query_count = queries.shape[0]
    model_width = queries.shape[1]
    head_count = HEADS
    head_size = model_width // head_count
    score_scale = head_size ** (-0.5)
    all_latents = lax.all_gather(latents, ("wide", "narrow"), axis=0, tiled=True)
    hidden = queries
    for layer_index in range(LAYERS):
        normed = layer_norm(hidden, norm_gains[layer_index])
        query_sums = project_queries(normed, q_weight[layer_index])
        query_rows = (query_sums * score_scale).astype(jnp.bfloat16)
        query_heads = query_rows.reshape(query_count, head_count, head_size)
        initial = (
            jnp.full((head_count, query_count), -1e30, jnp.float32),
            jnp.zeros((head_count, query_count), jnp.float32),
            jnp.zeros((query_count, head_count, head_size), jnp.float32),
        )
        key_rows, value_rows = project_latents(
            all_latents, k_weight[layer_index], v_weight[layer_index]
        )
        carried = attend_rows(initial, (key_rows, value_rows), query_heads)
        row_max, row_sum, weighted = carried
        attended = (
            (weighted / jnp.transpose(row_sum)[:, :, None])
            .reshape(query_count, model_width)
            .astype(jnp.bfloat16)
        )
        output_rows = project_output(attended, o_weight[layer_index])
        hidden = (hidden.astype(jnp.float32) + output_rows).astype(jnp.bfloat16)
    return hidden


def solution(mesh):
    return jax.shard_map(
        shards,
        mesh=mesh,
        in_specs=(
            P(("groups", "wide", "narrow"), None),
            P(("groups", "wide", "narrow"), None),
            P(),
            P(None, "narrow", None),
            P(None, "narrow", None),
            P(None, "narrow", None),
            P(None, "narrow", None),
        ),
        out_specs=P(("groups", "wide", "narrow"), None),
        check_vma=False,
    )
```

profile of v0, /device:TPU:0, one launch (start us, length us, event | category | flops | bytes accessed | tf_op | source)
XLA Modules:
  0.0 126.7 jit_solution(10234056180179298440)
XLA Ops:
  6.5 3.2 %fusion.77 = (bf16[1,512,1024]{2,1,0:T(8,128)(2,1)}, bf16[1,512,1024]{2,1,0:T(8,128)(2,1)}) fusion(bf16[2,512,1024]{2,1,0:T(8,128)(2,1)} %param.12), kind=kLoop, calls=%fused_computation.75 | loop fusion | bytes 4194304 | tf_op jit(solution)/shard_map/slice | solution.py:98
  9.8 1.5 %fusion.76 = (bf16[1,512,1024]{2,1,0:T(8,128)(2,1)}, bf16[1,512,1024]{2,1,0:T(8,128)(2,1)}) fusion(bf16[2,512,1024]{2,1,0:T(8,128)(2,1)S(1)} %copy-done.2), kind=kLoop, calls=%fused_computation.74 | loop fusion | bytes 4194304 | tf_op jit(solution)/shard_map/slice | solution.py:89
  11.4 3.1 %fusion.75 = (bf16[1,512,1024]{2,1,0:T(8,128)(2,1)}, bf16[1,512,1024]{2,1,0:T(8,128)(2,1)}) fusion(bf16[2,512,1024]{2,1,0:T(8,128)(2,1)} %param.11), kind=kLoop, calls=%fused_computation.73 | loop fusion | bytes 4194304 | tf_op jit(solution)/shard_map/slice | solution.py:98
  15.1 0.9 copy-done.3
  16.1 1.5 %fusion.74 = (bf16[1,512,1024]{2,1,0:T(8,128)(2,1)}, bf16[1,512,1024]{2,1,0:T(8,128)(2,1)}) fusion(bf16[2,512,1024]{2,1,0:T(8,128)(2,1)S(1)} %copy-done.3), kind=kLoop, calls=%fused_computation.72 | loop fusion | bytes 4194304 | tf_op jit(solution)/shard_map/slice | solution.py:107
  19.7 23.8 %all_gather.28 = bf16[128,1024]{1,0:T(8,128)(2,1)S(1)} all-gather(bf16[8,1024]{1,0:T(8,128)(2,1)S(1)} %copy-done.5), channel_id=1, replica_groups=mesh['groups'=2,'wide'=8,'narrow'=2] {'wide','narrow'}, dimensions={0}, use_global_device_ids=true | all-gather | bytes 278528 | tf_op jit(solution)/shard_map/all_gather | solution.py:85
  44.2 2.2 %fusion.57 = bf16[128,1024]{1,0:T(8,128)(2,1)S(1)} fusion(bf16[128,1024]{1,0:T(8,128)(2,1)S(1)} %all_gather.28, bf16[1,1024,1024]{2,1,0:T(8,128)(2,1)} %all-gather.21.cloned.1.call-done), kind=kOutput, calls=%fused_computation.53 | convolution fusion | flops 268566528 | bytes 2621440 | tf_op jit(solution)/shard_map/dot_general | solution.py:20
  46.4 0.9 copy.18
  47.3 3.2 %multiply_convert_fusion.1 = bf16[512,1024]{1,0:T(8,128)(2,1)S(1)} fusion(bf16[1,1024,1024]{2,1,0:T(8,128)(2,1)} %all-gather.17.cloned.1.call-done, bf16[512,1024]{1,0:T(8,128)(2,1)S(1)} %copy-done.1, f32[1024]{0:T(1024)S(1)} %bitcast.95, f32[512]{0:T(512)S(1)} %add_rsqrt_fusion.1, f32[512]{0:T(512)S(1)} %broadcast_multiply_fusion.1), kind=kOutput, calls=%fused_computation.51 | convolution fusion | flops 1077411840 | bytes 4202496 | tf_op jit(solution)/shard_map/dot_general | solution.py:20
  51.1 2.0 %fusion.54 = bf16[128,1024]{1,0:T(8,128)(2,1)S(1)} fusion(bf16[128,1024]{1,0:T(8,128)(2,1)S(1)} %all_gather.28, bf16[1,1024,1024]{2,1,0:T(8,128)(2,1)} %all-gather.19.cloned.1.call-done), kind=kOutput, calls=%fused_computation.52 | convolution fusion | flops 268566528 | bytes 2621440 | tf_op jit(solution)/shard_map/dot_general | solution.py:20
  54.8 1.2 copy-done
  56.0 7.0 %all-gather.29.cloned.1.call-done = bf16[1,1024,1024]{2,1,0:T(8,128)(2,1)} async-done(((bf16[1,512,1024]{2,1,0:T(8,128)(2,1)}), bf16[1,1024,1024]{2,1,0:T(8,128)(2,1)}) %all-gather.29.cloned.1.call-update) | async-done | bytes 2097168 | tf_op jit(solution)/shard_map/all_gather | solution.py:43
  63.1 2.0 %fusion.63 = bf16[128,1024]{1,0:T(8,128)(2,1)S(1)} fusion(bf16[128,1024]{1,0:T(8,128)(2,1)S(1)} %all_gather.28, bf16[1,1024,1024]{2,1,0:T(8,128)(2,1)} %all-gather.29.cloned.1.call-done), kind=kOutput, calls=%fused_computation.55 | convolution fusion | flops 268566528 | bytes 2621440 | tf_op jit(solution)/shard_map/dot_general | solution.py:20
  65.3 4.1 %fusion.33 = bf16[512,16,64]{0,2,1:T(8,128)(2,1)} fusion(bf16[128,16,64]{0,2,1:T(8,128)(2,1)S(1)} %bitcast.93, f32[16,512,128]{1,2,0:T(8,128)} %copy-done, f32[16,512]{1,0:T(8,128)S(1)} %get-tuple-element.56, f32[512,16]{0,1:T(8,128)S(1)} %bitcast_add_fusion.3, f32[512,16]{0,1:T(8,128)S(1)} %get-tuple-element.48), kind=kOutput, calls=%fused_computation.41 | convolution fusion | flops 137887744 | bytes 5603328 | tf_op jit(solution)/shard_map/while/body/eval_jaxpr/hqk,khd->qhd/dot_general | solution.py:66
  69.4 6.9 %all-gather.23.cloned.1.call-done = bf16[1,1024,1024]{2,1,0:T(8,128)(2,1)} async-done(((bf16[1,512,1024]{2,1,0:T(8,128)(2,1)}), bf16[1,1024,1024]{2,1,0:T(8,128)(2,1)}) %all-gather.23.cloned.1.call-update) | async-done | bytes 2097168 | tf_op jit(solution)/shard_map/all_gather | solution.py:38
  76.2 3.3 %convert_reduce_fusion = (f32[512]{0:T(512)S(1)}, bf16[512,1024]{1,0:T(8,128)(2,1)S(1)}) fusion(bf16[512,1024]{0,1:T(8,128)(2,1)} %bitcast.96, bf16[1,1024,1024]{2,1,0:T(8,128)(2,1)} %all-gather.23.cloned.1.call-done, bf16[512,1024]{1,0:T(8,128)(2,1)S(1)} %copy-done.1), kind=kOutput, calls=%fused_computation.8 | convolution fusion | flops 1076362752 | bytes 5244928 | tf_op jit(solution)/shard_map/dot_general | solution.py:20
  79.9 9.5 %all-gather.25.cloned.1.call-done = bf16[1,1024,1024]{2,1,0:T(8,128)(2,1)} async-done(((bf16[1,512,1024]{2,1,0:T(8,128)(2,1)}), bf16[1,1024,1024]{2,1,0:T(8,128)(2,1)}) %all-gather.25.cloned.1.call-update) | async-done | bytes 2097168 | tf_op jit(solution)/shard_map/all_gather | solution.py:29
  89.4 3.9 %multiply_convert_fusion = bf16[512,1024]{1,0:T(8,128)(2,1)} fusion(bf16[1,1024,1024]{2,1,0:T(8,128)(2,1)} %all-gather.25.cloned.1.call-done, bf16[512,1024]{1,0:T(8,128)(2,1)S(1)} %get-tuple-element.64, f32[1024]{0:T(1024)S(1)} %bitcast.94, f32[512]{0:T(512)S(1)} %add_rsqrt_fusion, f32[512]{0:T(512)S(1)} %broadcast_multiply_fusion), kind=kOutput, calls=%fused_computation.49 | convolution fusion | flops 1077411840 | bytes 4202496 | tf_op jit(solution)/shard_map/dot_general | solution.py:20
  93.3 1.5 %copy.20 = bf16[512,1024]{0,1:T(8,128)(2,1)S(1)} copy(bf16[512,1024]{1,0:T(8,128)(2,1)} %multiply_convert_fusion) | data formatting | bytes 2097152 | tf_op jit(solution)/shard_map/convert_element_type | solution.py:90
  94.8 8.0 %all-gather.27.cloned.1.call-done = bf16[1,1024,1024]{2,1,0:T(8,128)(2,1)} async-done(((bf16[1,512,1024]{2,1,0:T(8,128)(2,1)}), bf16[1,1024,1024]{2,1,0:T(8,128)(2,1)}) %all-gather.27.cloned.1.call-update) | async-done | bytes 2097168 | tf_op jit(solution)/shard_map/all_gather | solution.py:42
  102.7 2.0 %fusion.60 = bf16[128,1024]{1,0:T(8,128)(2,1)S(1)} fusion(bf16[128,1024]{1,0:T(8,128)(2,1)S(1)} %all_gather.28, bf16[1,1024,1024]{2,1,0:T(8,128)(2,1)} %all-gather.27.cloned.1.call-done), kind=kOutput, calls=%fused_computation.54 | convolution fusion | flops 268566528 | bytes 2621440 | tf_op jit(solution)/shard_map/dot_general | solution.py:20
  106.5 1.0 fusion.23
  107.5 8.6 %all-gather.31.cloned.1.call-done = bf16[1,1024,1024]{2,1,0:T(8,128)(2,1)} async-done(((bf16[1,512,1024]{2,1,0:T(8,128)(2,1)}), bf16[1,1024,1024]{2,1,0:T(8,128)(2,1)}) %all-gather.31.cloned.1.call-update) | async-done | bytes 2097168 | tf_op jit(solution)/shard_map/all_gather | solution.py:38
  116.1 3.8 %fusion.15 = bf16[512,1024]{1,0:T(8,128)(2,1)} fusion(bf16[512,1024]{1,0:T(8,128)(2,1)S(1)} %get-tuple-element.64, bf16[512,1024]{0,1:T(8,128)(2,1)S(1)} %bitcast.97, bf16[1,1024,1024]{2,1,0:T(8,128)(2,1)} %all-gather.31.cloned.1.call-done), kind=kOutput, calls=%fused_computation.23 | convolution fusion | flops 1075314688 | bytes 5242880 | tf_op jit(solution)/shard_map/dot_general | solution.py:20
  (51 shorter events, 8.0 us)
Async XLA Ops:
  6.5 3.3 %copy-start.2 = (bf16[2,512,1024]{2,1,0:T(8,128)(2,1)S(1)}, bf16[2,512,1024]{2,1,0:T(8,128)(2,1)}, u32[]{:S(2)}) copy-start(bf16[2,512,1024]{2,1,0:T(8,128)(2,1)} %param.10) | copy-start | bytes 6291460
  6.5 37.6 %all-gather.21.cloned.1.call-start = ((), (), s32[]{:S(2)}) async-start(), calls=%async_computation.2 | async-start | bytes 3145728 | tf_op jit(solution)/shard_map/all_gather | solution.py:43
  9.8 37.5 %all-gather.17.cloned.1.call-start = ((), (), s32[]{:S(2)}) async-start(), calls=%async_computation | async-start | bytes 3145728 | tf_op jit(solution)/shard_map/all_gather | solution.py:29
  11.3 39.7 %all-gather.19.cloned.1.call-start = ((), (), s32[]{:S(2)}) async-start(), calls=%async_computation.1 | async-start | bytes 3145728 | tf_op jit(solution)/shard_map/all_gather | solution.py:42
  14.5 1.6 %copy-start.3 = (bf16[2,512,1024]{2,1,0:T(8,128)(2,1)S(1)}, bf16[2,512,1024]{2,1,0:T(8,128)(2,1)}, u32[]{:S(2)}) copy-start(bf16[2,512,1024]{2,1,0:T(8,128)(2,1)} %param.13) | copy-start | bytes 6291460
  14.5 48.6 %all-gather.29.cloned.1.call-start = ((), (), s32[]{:S(2)}) async-start(), calls=%async_computation.6 | async-start | bytes 3145728 | tf_op jit(solution)/shard_map/all_gather | solution.py:43
  15.1 61.2 %all-gather.23.cloned.1.call-start = ((), (), s32[]{:S(2)}) async-start(), calls=%async_computation.3 | async-start | bytes 3145728 | tf_op jit(solution)/shard_map/all_gather | solution.py:38
  17.5 2.1 %copy-start.5 = (bf16[8,1024]{1,0:T(8,128)(2,1)S(1)}, bf16[8,1024]{1,0:T(8,128)(2,1)}, u32[]{:S(2)}) copy-start(bf16[8,1024]{1,0:T(8,128)(2,1)} %param.8) | copy-start | bytes 49156
  17.6 25.9 %copy-start.6 = (f32[2,1024]{1,0:T(2,128)S(1)}, f32[2,1024]{1,0:T(2,128)}, u32[]{:S(2)}) copy-start(f32[2,1024]{1,0:T(2,128)} %param.9) | copy-start | bytes 24580
  17.6 25.9 %copy-start.1 = (bf16[512,1024]{1,0:T(8,128)(2,1)S(1)}, bf16[512,1024]{1,0:T(8,128)(2,1)}, u32[]{:S(2)}) copy-start(bf16[512,1024]{1,0:T(8,128)(2,1)} %param.7) | copy-start | bytes 3145732
  17.6 71.8 %all-gather.25.cloned.1.call-start = ((), (), s32[]{:S(2)}) async-start(), calls=%async_computation.4 | async-start | bytes 3145728 | tf_op jit(solution)/shard_map/all_gather | solution.py:29
  18.2 84.6 %all-gather.27.cloned.1.call-start = ((), (), s32[]{:S(2)}) async-start(), calls=%async_computation.5 | async-start | bytes 3145728 | tf_op jit(solution)/shard_map/all_gather | solution.py:42
  18.9 97.2 %all-gather.31.cloned.1.call-start = ((), (), s32[]{:S(2)}) async-start(), calls=%async_computation.7 | async-start | bytes 3145728 | tf_op jit(solution)/shard_map/all_gather | solution.py:38
  54.1 2.0 %copy-start = (f32[16,512,128]{1,2,0:T(8,128)}, f32[16,512,128]{1,2,0:T(8,128)S(1)}, u32[]{:S(2)}) copy-start(f32[16,512,128]{1,2,0:T(8,128)S(1)} %get-tuple-element.62) | copy-start | bytes 12582916
  56.0 9.2 %copy-start.4 = (bf16[128,1024]{0,1:T(8,128)(2,1)S(1)}, bf16[128,1024]{0,1:T(8,128)(2,1)}, u32[]{:S(2)}) copy-start(bf16[128,1024]{0,1:T(8,128)(2,1)} %copy.18) | copy-start | bytes 786436
Sparse Core Ops, SparseCore 0:
  9.9 13.2 all-gather.20
  24.8 11.7 all-gather.16
  38.1 11.7 all-gather.18
  51.3 11.7 all-gather.28
  64.4 11.7 all-gather.22
  77.6 11.7 all-gather.24
  91.0 11.7 all-gather.26
  104.3 11.7 all-gather.30
where the time goes:
time: 127 us
  waiting for transfers between devices  42.4 us (33%)
  matrix products  29.1 us (23%)
  blocking collectives  23.8 us (19%)
  local copies, waits for them, and re-layouts  14.9 us (12%)
  between operations  13.7 us (11%)
  other arithmetic  2.53 us (2%)
    all_gather x1, blocking collectives, shards(): lax.all_gather(latents, ('wide', 'narrow'), axis=0, tiled=True)  23.8 us
    dot_general x8, matrix products, accumulate(): return jnp.dot(left_rows, panel_piece, preferred_element_type=jnp.float32)  22.5 us
    all_gather x2, waiting for transfers between devices, project_output(): lax.all_gather(panel, 'narrow', axis=0, tiled=True)  15.5 us
    all_gather x2, waiting for transfers between devices, project_queries(): lax.all_gather(panel, 'narrow', axis=0, tiled=True)  9.47 us
    all_gather x2, waiting for transfers between devices, project_latents(): lax.all_gather(key_panel, 'narrow', axis=0, tiled=True)  7.98 us
    all_gather x2, waiting for transfers between devices, project_latents(): lax.all_gather(value_panel, 'narrow', axis=0, tiled=True)  7.02 us
    dot_general x2, matrix products, fold_step(): jnp.einsum('hqk,khd->qhd', expo.astype(jnp.bfloat16), value_block, prefer...  5.08 us
    slice x1, local copies, waits for them, and re-layouts, shards(): v_weight[layer_index]  3.22 us
  transfers between devices with their start and end apart: 8, of which 5 were waited for; matrix products, arithmetic and copies ran while one was open for 29% of the time, Pallas kernels for 0%

commit v1 on v0

v1 whole, which is shorter than its diff:
```python
import functools

import jax
import jax.numpy as jnp
from jax import lax
from jax.experimental import pallas as pl
from jax.experimental.pallas import tpu as pltpu
from jax.sharding import PartitionSpec as P

HEADS = 16
LAYERS = 2
ANY = pl.BlockSpec(memory_space=pl.ANY)
VMEM = pl.BlockSpec(memory_space=pltpu.VMEM)
SMEM = pl.BlockSpec(memory_space=pltpu.SMEM)
GRANT = 24 * 2**20
LARGE_GRANT = 58 * 2**20


def layer_norm(row_data, gain):
    values = row_data.astype(jnp.float32)
    center = values - jnp.mean(values, axis=-1, keepdims=True)
    spread = jnp.mean(center * center, axis=-1, keepdims=True)
    return (center * lax.rsqrt(spread + 1e-05) * gain).astype(jnp.bfloat16)


def dot(left, right):
    return jnp.dot(left, right, preferred_element_type=jnp.float32)


def dot_t(left, right):
    return lax.dot_general(
        left, right, (((1,), (1,)), ((), ())), preferred_element_type=jnp.float32
    )


def split_dot(core, left, own, other):
    half = own.shape[0]
    mine = left[:, pl.ds(pl.multiple_of(core * half, half), half)]
    theirs = left[:, pl.ds(pl.multiple_of((1 - core) * half, half), half)]
    return dot(
        jnp.concatenate([mine, theirs], axis=1), jnp.concatenate([own[...], other[...]], axis=0)
    )


def fetch(core, own, other, target, sems):
    half = own.shape[0]
    copies = []
    for place, (source, number) in enumerate(((own, core), (other, 1 - core))):
        rows = pl.ds(pl.multiple_of(number * half, half), half)
        copies.append(pltpu.make_async_copy(source, target.at[rows], sems.at[place]))
    for copy in copies:
        copy.start()
    return copies


def finish(copies):
    for copy in copies:
        copy.wait()


def norm_kernel(hidden, gains, q_other, out, q_first, sem):
    copy = pltpu.make_async_copy(q_other.at[0], q_first, sem)
    copy.start()
    out[...] = layer_norm(hidden[...], gains[0:1, :])
    copy.wait()


def query_kernel(narrow, normed, q_own, q_other, out, *, scale, block):
    @pl.loop(0, normed.shape[0] // block)
    def _(step):
        rows = pl.ds(pl.multiple_of(step * block, block), block)
        query = split_dot(narrow[0], normed.at[rows, :], q_own.at[0], q_other)
        out[rows, :] = (query * scale).astype(jnp.bfloat16)


def latent_kernel(latents, k_own, v_own, first, second):
    for layer, target in enumerate((first, second)):
        for i, own in enumerate((k_own, v_own)):
            target[i] = dot(latents[...], own[layer])


def pair_up(mine, theirs, key_pairs, value_pairs):
    _, count, width = mine.shape
    low = lax.broadcasted_iota(jnp.int32, (count, 128), 1) < width // HEADS
    zero = jnp.zeros((count, 128), jnp.bfloat16)
    one = jnp.ones((count, 128), jnp.bfloat16)
    for pair in range(width // 128):
        columns = slice(pair * 128, pair * 128 + 128)
        for i, target in enumerate((key_pairs, value_pairs)):
            piece = (mine[i, :, columns] + theirs[i, :, columns]).astype(jnp.bfloat16)
            target[pair, 0:count, 0:128] = jnp.where(low, piece, zero)
            target[pair, count : 2 * count, 0:128] = jnp.where(low, zero, piece)
        value_pairs[pair, 0:count, 128:256] = jnp.where(low, one, zero)
        value_pairs[pair, count : 2 * count, 128:256] = jnp.where(low, zero, one)


def attend(query, key_pairs, value_pairs, attended):
    pairs, twice, _ = key_pairs.shape
    count = twice // 2
    for pair in range(pairs):
        columns = slice(pair * 128, pair * 128 + 128)
        scores = dot_t(query[:, columns], key_pairs[pair])
        expo = []
        for head in range(2):
            part = scores[:, head * count : (head + 1) * count]
            expo.append(jnp.exp(part - jnp.max(part, axis=-1, keepdims=True)).astype(jnp.bfloat16))
        mixed = dot(jnp.concatenate(expo, axis=1), value_pairs[pair])
        attended[:, columns] = (mixed[:, 0:128] / mixed[:, 128:256]).astype(jnp.bfloat16)


def add_output(state, attended, panel):
    return (state.astype(jnp.float32) + dot(attended, panel)).astype(jnp.bfloat16)


def attend_all(query, mine, theirs, key_pairs, value_pairs, attended, block):
    pair_up(mine, theirs, key_pairs, value_pairs)

    @pl.loop(0, query.shape[0] // block)
    def _(step):
        rows = pl.ds(pl.multiple_of(step * block, block), block)
        attend(query[rows, :], key_pairs, value_pairs, attended.at[rows, :])


def first_kernel(
    narrow, hidden, query, mine, theirs, gains, q_own, q_other, o_own, o_other, out, next_query,
    q_panel, o_panel, key_pairs, value_pairs, attended, sems, *, scale, block, dense_block,
):
    o_copies = fetch(narrow[0], o_own.at[0], o_other.at[0], o_panel, sems.at[0])
    q_copies = fetch(narrow[0], q_own.at[1], q_other.at[1], q_panel, sems.at[1])
    attend_all(query, mine, theirs, key_pairs, value_pairs, attended, block)
    finish(o_copies)
    finish(q_copies)

    @pl.loop(0, hidden.shape[0] // dense_block)
    def _(step):
        rows = pl.ds(pl.multiple_of(step * dense_block, dense_block), dense_block)
        state = add_output(hidden[rows, :], attended[rows, :], o_panel[...])
        out[rows, :] = state
        normed = layer_norm(state, gains[1:2, :])
        next_query[rows, :] = (dot(normed, q_panel[...]) * scale).astype(jnp.bfloat16)


def last_kernel(
    narrow, hidden, query, mine, theirs, o_own, o_other, out,
    o_panel, key_pairs, value_pairs, attended, result, sems, out_sems, *, block, chunk,
):
    copies = fetch(narrow[0], o_own.at[1], o_other.at[1], o_panel, sems)
    attend_all(query, mine, theirs, key_pairs, value_pairs, attended, block)
    finish(copies)
    leaving = []
    for step in range(hidden.shape[1] // chunk):
        columns = slice(step * chunk, step * chunk + chunk)
        result[:, columns] = add_output(hidden[:, columns], attended[...], o_panel[:, columns])
        leaving.append(
            pltpu.make_async_copy(result.at[:, columns], out.at[:, columns], out_sems.at[step])
        )
        leaving[-1].start()
    finish(leaving)


def make_shards(wide):
    def swap(array):
        return lax.ppermute(array, "narrow", [(0, 1), (1, 0)])

    def after(first, *others):
        return lax.optimization_barrier((first,) + others)

    def shards(queries, latents, norm_gains, q_weight, k_weight, v_weight, o_weight):
        core = lax.axis_index("narrow").astype(jnp.int32)
        narrow = core.reshape(1)
        rows, width = queries.shape
        count = latents.shape[0] * wide * 2
        scale = (width // HEADS) ** (-0.5)
        block = min(256, max(16, 32768 // count))
        params = pltpu.CompilerParams(vmem_limit_bytes=GRANT if count <= 256 else LARGE_GRANT)
        panel = pltpu.VMEM((width, width), jnp.bfloat16)
        attended = pltpu.VMEM((rows, width), jnp.bfloat16)
        pairs = [
            pltpu.VMEM((width // 128, 2 * count, 128), jnp.bfloat16),
            pltpu.VMEM((width // 128, 2 * count, 256), jnp.bfloat16),
        ]
        hidden_shape = jax.ShapeDtypeStruct((rows, width), jnp.bfloat16)
        dense = 2 * rows * width * width
        latent_cost = 4 * count * width * width
        attend_cost = 8 * rows * count * width

        def cost(flops, transcendentals=0):
            return pl.CostEstimate(
                flops=flops, bytes_accessed=4 * width * width, transcendentals=transcendentals
            )

        q_other = swap(q_weight)
        gathered = latents
        step = wide // 2
        while step > 1:
            received = lax.ppermute(gathered, "wide", [(i, i ^ step) for i in range(wide)])
            if step == wide // 2:
                received, q_other, o_weight = after(received, q_other, o_weight)
                o_other = swap(o_weight)
                normed, q_first = pl.pallas_call(
                    norm_kernel,
                    out_shape=(hidden_shape, jax.ShapeDtypeStruct((width // 2, width), jnp.bfloat16)),
                    in_specs=[VMEM, VMEM, ANY],
                    out_specs=(VMEM, VMEM),
                    scratch_shapes=[pltpu.SemaphoreType.DMA],
                    compiler_params=params,
                    cost_estimate=cost(dense),
                )(queries, norm_gains, q_other)
            if step == 2:
                received, normed = after(received, normed)
            gathered = jnp.concatenate([gathered, received], axis=0)
            step //= 2

        half = width // 2
        left, right = gathered[:, :half], gathered[:, half:]
        keep = jnp.where(core == 0, left, right)
        give = jnp.where(core == 0, right, left)
        keep, give = after(keep, give)
        devices = range(2 * wide)
        beside, along, across = (
            lax.ppermute(array, ("wide", "narrow"), [(i, i ^ mask) for i in devices])
            for mask, array in ((1, give), (2, keep), (3, give))
        )
        gathered = jnp.concatenate(
            [
                jnp.where(core == 0, keep, beside),
                jnp.where(core == 0, beside, keep),
                jnp.where(core == 0, along, across),
                jnp.where(core == 0, across, along),
            ],
            axis=0,
        )

        query = pl.pallas_call(
            functools.partial(query_kernel, scale=scale, block=rows),
            out_shape=hidden_shape,
            in_specs=[SMEM] + [VMEM] * 3,
            out_specs=VMEM,
            compiler_params=params,
            cost_estimate=cost(dense),
        )(narrow, normed, q_weight, q_first)
        gathered, query, o_other = after(gathered, query, o_other)

        partial_shape = jax.ShapeDtypeStruct((2, count, width), jnp.float32)
        first, second = pl.pallas_call(
            latent_kernel,
            out_shape=(partial_shape, partial_shape),
            in_specs=[VMEM] * 3,
            out_specs=(VMEM, VMEM),
            compiler_params=params,
            cost_estimate=cost(latent_cost),
        )(gathered, k_weight, v_weight)
        first_other = swap(first)
        first_other, second = after(first_other, second)
        second_other = swap(second)

        hidden, query = pl.pallas_call(
            functools.partial(first_kernel, scale=scale, block=block, dense_block=rows),
            out_shape=(hidden_shape, hidden_shape),
            in_specs=[SMEM] + [VMEM] * 5 + [ANY] * 4,
            out_specs=(VMEM, VMEM),
            scratch_shapes=[panel, panel] + pairs + [attended, pltpu.SemaphoreType.DMA((2, 2))],
            compiler_params=params,
            cost_estimate=cost(2 * dense + attend_cost, rows * count * HEADS),
        )(narrow, queries, query, first, first_other, norm_gains, q_weight, q_other, o_weight, o_other)
        return pl.pallas_call(
            functools.partial(last_kernel, block=block, chunk=256),
            out_shape=hidden_shape,
            in_specs=[SMEM] + [VMEM] * 4 + [ANY] * 2,
            out_specs=ANY,
            scratch_shapes=[panel]
            + pairs
            + [
                attended,
                pltpu.VMEM((rows, width), jnp.bfloat16),
                pltpu.SemaphoreType.DMA((2,)),
                pltpu.SemaphoreType.DMA((width // 256,)),
            ],
            compiler_params=params,
            cost_estimate=cost(attend_cost + dense, rows * count * HEADS),
        )(narrow, hidden, query, second, second_other, o_weight, o_other)

    return shards


def solution(mesh):
    rows = P(("groups", "wide", "narrow"), None)
    weight = P(None, "narrow", None)
    return jax.shard_map(
        make_shards(mesh.shape["wide"]),
        mesh=mesh,
        in_specs=(rows, rows, P(), weight, weight, weight, weight),
        out_specs=rows,
        check_vma=False,
    )
```

time: 127 us -> 34.6 us (0.27)
  waiting for transfers between devices: 42.4 us -> 6.66 us
  matrix products: 29.1 us -> 0 us
  blocking collectives: 23.8 us -> 0 us
  between operations: 13.7 us -> 0.16 us
  Pallas kernels: 0 us -> 12.7 us
  local copies, waits for them, and re-layouts: 14.9 us -> 5.6 us
  starting transfers between devices: 0.28 us -> 8.36 us
  other arithmetic: 2.53 us -> 0.76 us
    all_gather x8 -> x0, waiting for transfers between devices: 39.9 us -> none  [the longest x2 15.5 us: project_output(): lax.all_gather(panel, 'narrow', axis=0, tiled=True)]
    dot_general x12 -> x0, matrix products: 29.1 us -> none  [the longest x8 22.5 us: accumulate(): return jnp.dot(left_rows, panel_piece, preferred_element_type=jnp.float32)]
    all_gather x1 -> x0, blocking collectives: 23.8 us -> none  [shards(): lax.all_gather(latents, ('wide', 'narrow'), axis=0, tiled=True)]
    pallas_call x0 -> x5, Pallas kernels: none -> 12.7 us  [the longest x1 5.41 us: shards(): pl.pallas_call(functools.partial(first_kernel, scale=scale, block=block,...]
    slice x5 -> x0, local copies, waits for them, and re-layouts: 9.26 us -> none  [the longest x1 3.22 us: shards(): v_weight[layer_index]]
    ppermute x0 -> x9, starting transfers between devices: none -> 8.36 us  [the longest x2 5.5 us: shards(): lax.ppermute(gathered, 'wide', [(i, i ^ step) for i in range(wide)])]
    ppermute x0 -> x9, waiting for transfers between devices: none -> 6.66 us  [the longest x4 2.65 us: swap(): return lax.ppermute(array, 'narrow', [(0, 1), (1, 0)])]
    convert_element_type x6 -> x0, local copies, waits for them, and re-layouts: 3.41 us -> none  [the longest x2 2.04 us: shards(): query_rows = (query_sums * score_scale).astype(jnp.bfloat16)]
  transfers between devices with their start and end apart: 8 -> 9, of which waited for: 5 -> 3; matrix products, arithmetic and copies ran while one was open for 29% -> 4% of each run, Pallas kernels for 0% -> 22%
where the time goes in v1:
time: 34.6 us; the launch traced here: 34.2 us
  Pallas kernels  12.7 us (37%)
  starting transfers between devices  8.36 us (24%)
  waiting for transfers between devices  6.66 us (19%)
  local copies, waits for them, and re-layouts  5.6 us (16%)
  other arithmetic  0.76 us (2%)
    unnamed x22, local copies, waits for them, and re-layouts  5.6 us
    ppermute x2, starting transfers between devices, shards(): lax.ppermute(gathered, 'wide', [(i, i ^ step) for i in range(wide)])  5.5 us
    pallas_call x1, Pallas kernels, shards(): pl.pallas_call(functools.partial(first_kernel, scale=scale, block=block,...  5.41 us
    pallas_call x1, Pallas kernels, shards(): pl.pallas_call(functools.partial(last_kernel, block=block, chunk=256), ou...  4.49 us
    ppermute x4, waiting for transfers between devices, swap(): return lax.ppermute(array, 'narrow', [(0, 1), (1, 0)])  2.65 us
    ppermute x3, starting transfers between devices, shards(): lax.ppermute(array, ('wide', 'narrow'), [(i, i ^ mask) for i in devices])  2.21 us
    ppermute x3, waiting for transfers between devices, shards(): lax.ppermute(array, ('wide', 'narrow'), [(i, i ^ mask) for i in devices])  2.08 us
    ppermute x2, waiting for transfers between devices, shards(): lax.ppermute(gathered, 'wide', [(i, i ^ step) for i in range(wide)])  1.93 us
  transfers between devices with their start and end apart: 9, of which 3 were waited for; matrix products, arithmetic and copies ran while one was open for 4% of the time, Pallas kernels for 22%

profile of v1, /device:TPU:0, one launch (start us, length us, event | category | flops | bytes accessed | tf_op | source)
XLA Modules:
  0.0 34.2 jit_solution(12730121572692877806)
XLA Ops:
  0.0 0.5 %collective-permute-start.1 = (bf16[2,512,1024]{2,1,0:T(8,128)(2,1)}, bf16[2,512,1024]{2,1,0:T(8,128)(2,1)S(1)}, u32[]{:S(2)}, u32[]{:S(2)}) collective-permute-start(bf16[2,512,1024]{2,1,0:T(8,128)(2,1)} %q_own.3), channel_id=1, source_target_pairs={{0,1},{1,0},{2,3},{3,2},{4,5},{5,4},{6,7},{7,6},{8,9},{9,8},{10,11... | collective-permute-start | bytes 6291464 | tf_op jit(solution)/shard_map/ppermute | solution.py:163
  0.5 3.6 %collective-permute-start = (bf16[8,1024]{1,0:T(8,128)(2,1)}, bf16[8,1024]{1,0:T(8,128)(2,1)S(1)}, u32[]{:S(2)}, u32[]{:S(2)}) collective-permute-start(bf16[8,1024]{1,0:T(8,128)(2,1)} %param.8), channel_id=1, source_target_pairs={{0,8},{2,10},{4,12},{6,14},{8,0},{10,2},{12,4},{14,6},{1,9},{3,11}... | collective-permute-start | bytes 49160 | tf_op jit(solution)/shard_map/ppermute | solution.py:196
  4.0 1.9 %collective-permute-done = bf16[8,1024]{1,0:T(8,128)(2,1)S(1)} collective-permute-done((bf16[8,1024]{1,0:T(8,128)(2,1)}, bf16[8,1024]{1,0:T(8,128)(2,1)S(1)}, u32[]{:S(2)}, u32[]{:S(2)}) %collective-permute-start) | collective-permute-done | bytes 16416 | tf_op jit(solution)/shard_map/ppermute | solution.py:196
  6.0 1.3 %copy-done.4 = bf16[2,512,1024]{2,1,0:T(8,128)(2,1)} copy-done((bf16[2,512,1024]{2,1,0:T(8,128)(2,1)}, bf16[2,512,1024]{2,1,0:T(8,128)(2,1)S(1)}, u32[]{:S(2)}) %copy-start.4) | copy-done | bytes 2097176
  7.3 0.0 collective-permute-start.6
  7.3 0.7 %constant_dynamic-update-slice_fusion.2 = bf16[32,1024]{1,0:T(8,128)(2,1)S(1)} fusion(bf16[8,1024]{1,0:T(8,128)(2,1)} %param.8), kind=kLoop, calls=%fused_computation.10 | loop fusion | bytes 32768
  8.0 0.7 %pad_maximum_fusion.1 = bf16[16,1024]{1,0:T(8,128)(2,1)S(1)} fusion(bf16[8,1024]{1,0:T(8,128)(2,1)S(1)} %collective-permute-done, bf16[8,1024]{1,0:T(8,128)(2,1)} %param.8), kind=kLoop, calls=%fused_computation.1 | loop fusion | flops 65536 | bytes 65536 | tf_op jit(solution)/shard_map/concatenate | solution.py:211
  8.8 1.9 %collective-permute-start.2 = (bf16[16,1024]{1,0:T(8,128)(2,1)S(1)}, bf16[16,1024]{1,0:T(8,128)(2,1)S(1)}, u32[]{:S(2)}, u32[]{:S(2)}) collective-permute-start(bf16[16,1024]{1,0:T(8,128)(2,1)S(1)} %pad_maximum_fusion.1), channel_id=1, source_target_pairs={{0,4},{2,6},{4,0},{6,2},{8,12},{10,14},{12,8},{14,10},{1,5},{3,7},... | collective-permute-start | bytes 98312 | tf_op jit(solution)/shard_map/ppermute | solution.py:196
  10.7 1.6 %copy-done.5 = bf16[2,512,1024]{2,1,0:T(8,128)(2,1)S(1)} copy-done((bf16[2,512,1024]{2,1,0:T(8,128)(2,1)S(1)}, bf16[2,512,1024]{2,1,0:T(8,128)(2,1)}, u32[]{:S(2)}) %copy-start.5) | copy-done | bytes 2097176
  12.3 1.2 %copy-done.7 = bf16[512,1024]{1,0:T(8,128)(2,1)S(1)} copy-done((bf16[512,1024]{1,0:T(8,128)(2,1)S(1)}, bf16[512,1024]{1,0:T(8,128)(2,1)}, u32[]{:S(2)}) %copy-start.7) | copy-done | bytes 1048600
  13.5 0.7 %copy-done.9 = f32[2,1024]{1,0:T(2,128)S(1)} copy-done((f32[2,1024]{1,0:T(2,128)S(1)}, f32[2,1024]{1,0:T(2,128)}, u32[]{:S(2)}) %copy-start.9) | copy-done | bytes 8216
  14.2 0.8 %shard_map.73 = (bf16[512,1024]{1,0:T(8,128)(2,1)S(1)}, bf16[512,1024]{1,0:T(8,128)(2,1)S(1)}) custom-call(bf16[512,1024]{1,0:T(8,128)(2,1)S(1)} %copy-done.7, f32[2,1024]{1,0:T(2,128)S(1)} %copy-done.9, bf16[2,512,1024]{2,1,0:T(8,128)(2,1)S(1)} %copy-done.5), custom_call_target="tpu_custom_call" | custom-call | flops 1073741824 | bytes 4194304 | tf_op jit(solution)/shard_map/pallas_call | solution.py:200
  15.0 1.4 %collective-permute-start.5 = (bf16[32,512]{1,0:T(8,128)(2,1)S(1)}, bf16[32,512]{1,0:T(8,128)(2,1)S(1)}, u32[]{:S(2)}, u32[]{:S(2)}) collective-permute-start(bf16[32,512]{1,0:T(8,128)(2,1)S(1)} %get-tuple-element.28), channel_id=1, source_target_pairs={{0,3},{1,2},{2,1},{3,0},{4,7},{5,6},{6,5},{7,4},{8,11},{9,10},{10,... | collective-permute-start | bytes 98312 | tf_op jit(solution)/shard_map/ppermute | solution.py:221
  16.4 0.3 collective-permute-start.3
  16.7 0.5 %collective-permute-start.4 = (bf16[32,512]{1,0:T(8,128)(2,1)S(1)}, bf16[32,512]{1,0:T(8,128)(2,1)S(1)}, u32[]{:S(2)}, u32[]{:S(2)}) collective-permute-start(bf16[32,512]{1,0:T(8,128)(2,1)S(1)} %get-tuple-element.27), channel_id=1, source_target_pairs={{0,2},{1,3},{2,0},{3,1},{4,6},{5,7},{6,4},{7,5},{8,10},{9,11},{10,... | collective-permute-start | bytes 98312 | tf_op jit(solution)/shard_map/ppermute | solution.py:221
  17.2 1.3 %shard_map.74.query = bf16[512,1024]{1,0:T(8,128)(2,1)S(1)} custom-call(s32[1]{0:T(128)} %bitcast.narrow, bf16[512,1024]{1,0:T(8,128)(2,1)S(1)} %get-tuple-element.29.normed, bf16[2,512,1024]{2,1,0:T(8,128)(2,1)S(1)} %copy-done.1, bf16[512,1024]{1,0:T(8,128)(2,1)S(1)} %get-tuple-element.30.q_other), custom_call_target="tpu_custom_call" | custom-call | flops 1073741824 | bytes 4194304 | tf_op jit(solution)/shard_map/pallas_call | solution.py:234
  18.5 2.1 %collective-permute-done.4 = bf16[32,512]{1,0:T(8,128)(2,1)S(1)} collective-permute-done((bf16[32,512]{1,0:T(8,128)(2,1)S(1)}, bf16[32,512]{1,0:T(8,128)(2,1)S(1)}, u32[]{:S(2)}, u32[]{:S(2)}) %collective-permute-start.4) | collective-permute-done | bytes 32800 | tf_op jit(solution)/shard_map/ppermute | solution.py:221
  20.6 0.0 copy-start
  20.7 0.8 %shard_map.75 = (f32[2,128,1024]{2,1,0:T(8,128)S(1)}, f32[2,128,1024]{2,1,0:T(8,128)S(1)}) custom-call(bf16[128,512]{1,0:T(8,128)(2,1)S(1)} %pad_maximum_fusion.latents, bf16[2,512,1024]{2,1,0:T(8,128)(2,1)S(1)} %copy-done.2, bf16[2,512,1024]{2,1,0:T(8,128)(2,1)S(1)} %copy-done.3), custom_call_target="tpu_custom_call" | custom-call | flops 536870912 | bytes 4194304 | tf_op jit(solution)/shard_map/pallas_call | solution.py:245
  21.4 0.1 collective-permute-start.7
  21.5 2.6 %collective-permute-done.7.theirs = f32[2,128,1024]{2,1,0:T(8,128)S(1)} collective-permute-done((f32[2,128,1024]{2,1,0:T(8,128)S(1)}, f32[2,128,1024]{2,1,0:T(8,128)S(1)}, u32[]{:S(2)}, u32[]{:S(2)}) %collective-permute-start.7) | collective-permute-done | bytes 1048608 | tf_op jit(solution)/shard_map/ppermute | solution.py:163
  24.2 0.1 collective-permute-start.8
  24.3 5.4 %shard_map.76 = (bf16[512,1024]{1,0:T(8,128)(2,1)S(1)}, bf16[512,1024]{1,0:T(8,128)(2,1)S(1)}) custom-call(s32[1]{0:T(128)} %bitcast.narrow, bf16[512,1024]{1,0:T(8,128)(2,1)S(1)} %copy-done.8, bf16[512,1024]{1,0:T(8,128)(2,1)S(1)} %shard_map.74.query, f32[2,128,1024]{2,1,0:T(8,128)S(1)} %get-tuple-element.34.mine, ...), custom_call_target="tpu_custom_call" | custom-call | flops 2684354560 | bytes 4194304 | tf_op jit(solution)/shard_map/pallas_call | solution.py:257
  29.7 4.5 %shard_map.77 = bf16[512,1024]{1,0:T(8,128)(2,1)} custom-call(s32[1]{0:T(128)} %bitcast.narrow, bf16[512,1024]{1,0:T(8,128)(2,1)S(1)} %get-tuple-element.38.hidden, bf16[512,1024]{1,0:T(8,128)(2,1)S(1)} %get-tuple-element.39.query, f32[2,128,1024]{2,1,0:T(8,128)S(1)} %get-tuple-element.40.mine, f32[2,128,1024]{2,1,0:T(8,128)S(1)} %collective-permute-done.8.theirs, ...), custom_call_target="tpu_custom_call" | custom-call | flops 1610612736 | bytes 4194304 | tf_op jit(solution)/shard_map/pallas_call | solution.py:266
  (27 shorter events, 0.1 us)
Async XLA Ops:
  0.0 6.0 %collective-permute-start.1 = (bf16[2,512,1024]{2,1,0:T(8,128)(2,1)}, bf16[2,512,1024]{2,1,0:T(8,128)(2,1)S(1)}, u32[]{:S(2)}, u32[]{:S(2)}) collective-permute-start(bf16[2,512,1024]{2,1,0:T(8,128)(2,1)} %q_own.3), channel_id=1, source_target_pairs={{0,1},{1,0},{2,3},{3,2},{4,5},{5,4},{6,7},{7,6},{8,9},{9,8},{10,11... | collective-permute-start | bytes 6291464 | tf_op jit(solution)/shard_map/ppermute | solution.py:163
  0.5 5.5 %collective-permute-start = (bf16[8,1024]{1,0:T(8,128)(2,1)}, bf16[8,1024]{1,0:T(8,128)(2,1)S(1)}, u32[]{:S(2)}, u32[]{:S(2)}) collective-permute-start(bf16[8,1024]{1,0:T(8,128)(2,1)} %param.8), channel_id=1, source_target_pairs={{0,8},{2,10},{4,12},{6,14},{8,0},{10,2},{12,4},{14,6},{1,9},{3,11}... | collective-permute-start | bytes 49160 | tf_op jit(solution)/shard_map/ppermute | solution.py:196
  6.0 1.3 %copy-start.4 = (bf16[2,512,1024]{2,1,0:T(8,128)(2,1)}, bf16[2,512,1024]{2,1,0:T(8,128)(2,1)S(1)}, u32[]{:S(2)}) copy-start(bf16[2,512,1024]{2,1,0:T(8,128)(2,1)S(1)} %collective-permute-done.1.q_other) | copy-start | bytes 6291460
  7.3 13.3 %collective-permute-start.6 = (bf16[2,512,1024]{2,1,0:T(8,128)(2,1)}, bf16[2,512,1024]{2,1,0:T(8,128)(2,1)S(1)}, u32[]{:S(2)}, u32[]{:S(2)}) collective-permute-start(bf16[2,512,1024]{2,1,0:T(8,128)(2,1)} %o_own.1), channel_id=1, source_target_pairs={{0,1},{1,0},{2,3},{3,2},{4,5},{5,4},{6,7},{7,6},{8,9},{9,8},{10,11... | collective-permute-start | bytes 6291464 | tf_op jit(solution)/shard_map/ppermute | solution.py:163
  8.8 6.2 %collective-permute-start.2 = (bf16[16,1024]{1,0:T(8,128)(2,1)S(1)}, bf16[16,1024]{1,0:T(8,128)(2,1)S(1)}, u32[]{:S(2)}, u32[]{:S(2)}) collective-permute-start(bf16[16,1024]{1,0:T(8,128)(2,1)S(1)} %pad_maximum_fusion.1), channel_id=1, source_target_pairs={{0,4},{2,6},{4,0},{6,2},{8,12},{10,14},{12,8},{14,10},{1,5},{3,7},... | collective-permute-start | bytes 98312 | tf_op jit(solution)/shard_map/ppermute | solution.py:196
  10.7 1.6 %copy-start.5 = (bf16[2,512,1024]{2,1,0:T(8,128)(2,1)S(1)}, bf16[2,512,1024]{2,1,0:T(8,128)(2,1)}, u32[]{:S(2)}) copy-start(bf16[2,512,1024]{2,1,0:T(8,128)(2,1)} %copy-done.4) | copy-start | bytes 6291460
  12.3 1.2 %copy-start.7 = (bf16[512,1024]{1,0:T(8,128)(2,1)S(1)}, bf16[512,1024]{1,0:T(8,128)(2,1)}, u32[]{:S(2)}) copy-start(bf16[512,1024]{1,0:T(8,128)(2,1)} %hidden.3) | copy-start | bytes 3145732
  13.5 0.7 %copy-start.9 = (f32[2,1024]{1,0:T(2,128)S(1)}, f32[2,1024]{1,0:T(2,128)}, u32[]{:S(2)}) copy-start(f32[2,1024]{1,0:T(2,128)} %gains.3) | copy-start | bytes 24580
  14.2 3.0 %copy-start.1 = (bf16[2,512,1024]{2,1,0:T(8,128)(2,1)S(1)}, bf16[2,512,1024]{2,1,0:T(8,128)(2,1)}, u32[]{:S(2)}) copy-start(bf16[2,512,1024]{2,1,0:T(8,128)(2,1)} %q_own.3) | copy-start | bytes 6291460
  15.0 5.6 %collective-permute-start.5 = (bf16[32,512]{1,0:T(8,128)(2,1)S(1)}, bf16[32,512]{1,0:T(8,128)(2,1)S(1)}, u32[]{:S(2)}, u32[]{:S(2)}) collective-permute-start(bf16[32,512]{1,0:T(8,128)(2,1)S(1)} %get-tuple-element.28), channel_id=1, source_target_pairs={{0,3},{1,2},{2,1},{3,0},{4,7},{5,6},{6,5},{7,4},{8,11},{9,10},{10,... | collective-permute-start | bytes 98312 | tf_op jit(solution)/shard_map/ppermute | solution.py:221
  16.4 2.1 %collective-permute-start.3 = (bf16[32,512]{1,0:T(8,128)(2,1)S(1)}, bf16[32,512]{1,0:T(8,128)(2,1)S(1)}, u32[]{:S(2)}, u32[]{:S(2)}) collective-permute-start(bf16[32,512]{1,0:T(8,128)(2,1)S(1)} %get-tuple-element.28), channel_id=1, source_target_pairs={{0,1},{1,0},{2,3},{3,2},{4,5},{5,4},{6,7},{7,6},{8,9},{9,8},{10,11... | collective-permute-start | bytes 98312 | tf_op jit(solution)/shard_map/ppermute | solution.py:221
  16.7 3.9 %collective-permute-start.4 = (bf16[32,512]{1,0:T(8,128)(2,1)S(1)}, bf16[32,512]{1,0:T(8,128)(2,1)S(1)}, u32[]{:S(2)}, u32[]{:S(2)}) collective-permute-start(bf16[32,512]{1,0:T(8,128)(2,1)S(1)} %get-tuple-element.27), channel_id=1, source_target_pairs={{0,2},{1,3},{2,0},{3,1},{4,6},{5,7},{6,4},{7,5},{8,10},{9,11},{10,... | collective-permute-start | bytes 98312 | tf_op jit(solution)/shard_map/ppermute | solution.py:221
  17.2 3.4 %copy-start.2 = (bf16[2,512,1024]{2,1,0:T(8,128)(2,1)S(1)}, bf16[2,512,1024]{2,1,0:T(8,128)(2,1)}, u32[]{:S(2)}) copy-start(bf16[2,512,1024]{2,1,0:T(8,128)(2,1)} %k_own.1) | copy-start | bytes 6291460
  17.2 3.5 %copy-start.3 = (bf16[2,512,1024]{2,1,0:T(8,128)(2,1)S(1)}, bf16[2,512,1024]{2,1,0:T(8,128)(2,1)}, u32[]{:S(2)}) copy-start(bf16[2,512,1024]{2,1,0:T(8,128)(2,1)} %v_own.1) | copy-start | bytes 6291460
  17.2 7.1 %copy-start.8 = (bf16[512,1024]{1,0:T(8,128)(2,1)S(1)}, bf16[512,1024]{1,0:T(8,128)(2,1)}, u32[]{:S(2)}) copy-start(bf16[512,1024]{1,0:T(8,128)(2,1)} %hidden.3) | copy-start | bytes 3145732
  20.6 3.7 %copy-start = (bf16[2,512,1024]{2,1,0:T(8,128)(2,1)S(1)}, bf16[2,512,1024]{2,1,0:T(8,128)(2,1)}, u32[]{:S(2)}) copy-start(bf16[2,512,1024]{2,1,0:T(8,128)(2,1)} %o_own.1) | copy-start | bytes 6291460
  20.6 3.7 %copy-start.6 = (bf16[2,512,1024]{2,1,0:T(8,128)(2,1)S(1)}, bf16[2,512,1024]{2,1,0:T(8,128)(2,1)}, u32[]{:S(2)}) copy-start(bf16[2,512,1024]{2,1,0:T(8,128)(2,1)} %copy-done.4) | copy-start | bytes 6291460
  21.4 2.7 %collective-permute-start.7 = (f32[2,128,1024]{2,1,0:T(8,128)S(1)}, f32[2,128,1024]{2,1,0:T(8,128)S(1)}, u32[]{:S(2)}, u32[]{:S(2)}) collective-permute-start(f32[2,128,1024]{2,1,0:T(8,128)S(1)} %get-tuple-element.34.mine), channel_id=1, source_target_pairs={{0,1},{1,0},{2,3},{3,2},{4,5},{5,4},{6,7},{7,6},{8,9},{9,8},{10,11... | collective-permute-start | bytes 3145736 | tf_op jit(solution)/shard_map/ppermute | solution.py:163
  24.2 5.6 %collective-permute-start.8 = (f32[2,128,1024]{2,1,0:T(8,128)S(1)}, f32[2,128,1024]{2,1,0:T(8,128)S(1)}, u32[]{:S(2)}, u32[]{:S(2)}) collective-permute-start(f32[2,128,1024]{2,1,0:T(8,128)S(1)} %get-tuple-element.40.mine), channel_id=1, source_target_pairs={{0,1},{1,0},{2,3},{3,2},{4,5},{5,4},{6,7},{7,6},{8,9},{9,8},{10,11... | collective-permute-start | bytes 3145736 | tf_op jit(solution)/shard_map/ppermute | solution.py:163

commit v2 on v1

--- a/solution.py
+++ b/solution.py
@@ -40,6 +40,14 @@
     return dot(
         jnp.concatenate([mine, theirs], axis=1), jnp.concatenate([own[...], other[...]], axis=0)
     )
+
+
+def start_kernel(latents, out, ones):
+    out[...] = latents[...]
+    twice = ones.shape[0]
+    first_row = lax.broadcasted_iota(jnp.int32, ones.shape, 0) < twice // 2
+    left_column = lax.broadcasted_iota(jnp.int32, ones.shape, 1) < 64
+    ones[...] = jnp.where(first_row == left_column, 1.0, 0.0).astype(jnp.bfloat16)
 
 
 def fetch(core, own, other, target, sems):
@@ -83,18 +91,15 @@
     _, count, width = mine.shape
     low = lax.broadcasted_iota(jnp.int32, (count, 128), 1) < width // HEADS
     zero = jnp.zeros((count, 128), jnp.bfloat16)
-    one = jnp.ones((count, 128), jnp.bfloat16)
     for pair in range(width // 128):
         columns = slice(pair * 128, pair * 128 + 128)
         for i, target in enumerate((key_pairs, value_pairs)):
             piece = (mine[i, :, columns] + theirs[i, :, columns]).astype(jnp.bfloat16)
             target[pair, 0:count, 0:128] = jnp.where(low, piece, zero)
             target[pair, count : 2 * count, 0:128] = jnp.where(low, zero, piece)
-        value_pairs[pair, 0:count, 128:256] = jnp.where(low, one, zero)
-        value_pairs[pair, count : 2 * count, 128:256] = jnp.where(low, zero, one)
-
-
-def attend(query, key_pairs, value_pairs, attended):
+
+
+def attend(query, ones, key_pairs, value_pairs, attended):
     pairs, twice, _ = key_pairs.shape
     count = twice // 2
     for pair in range(pairs):
@@ -104,30 +109,40 @@
         for head in range(2):
             part = scores[:, head * count : (head + 1) * count]
             expo.append(jnp.exp(part - jnp.max(part, axis=-1, keepdims=True)).astype(jnp.bfloat16))
-        mixed = dot(jnp.concatenate(expo, axis=1), value_pairs[pair])
-        attended[:, columns] = (mixed[:, 0:128] / mixed[:, 128:256]).astype(jnp.bfloat16)
+        weights = jnp.concatenate([value_pairs[pair], ones[...]], axis=1)
+        mixed = dot(jnp.concatenate(expo, axis=1), weights)
+        sums = mixed[:, 128:256]
+        inverse = pl.reciprocal(sums, approx=True)
+        inverse = inverse * (2.0 - sums * inverse)
+        attended[:, columns] = (mixed[:, 0:128] * inverse).astype(jnp.bfloat16)
 
 
 def add_output(state, attended, panel):
     return (state.astype(jnp.float32) + dot(attended, panel)).astype(jnp.bfloat16)
 
 
-def attend_all(query, mine, theirs, key_pairs, value_pairs, attended, block):
+def attend_all(query, ones, mine, theirs, key_pairs, value_pairs, attended, block):
     pair_up(mine, theirs, key_pairs, value_pairs)
-
-    @pl.loop(0, query.shape[0] // block)
-    def _(step):
+    steps = query.shape[0] // block
+
+    def one_block(step):
         rows = pl.ds(pl.multiple_of(step * block, block), block)
-        attend(query[rows, :], key_pairs, value_pairs, attended.at[rows, :])
+        attend(query[rows, :], ones, key_pairs, value_pairs, attended.at[rows, :])
+
+    if steps <= 2:
+        for step in range(steps):
+            one_block(step)
+    else:
+        pl.loop(0, steps)(one_block)
 
 
 def first_kernel(
-    narrow, hidden, query, mine, theirs, gains, q_own, q_other, o_own, o_other, out, next_query,
+    narrow, hidden, query, ones, mine, theirs, gains, q_own, q_other, o_own, o_other, out, next_query,
     q_panel, o_panel, key_pairs, value_pairs, attended, sems, *, scale, block, dense_block,
 ):
     o_copies = fetch(narrow[0], o_own.at[0], o_other.at[0], o_panel, sems.at[0])
     q_copies = fetch(narrow[0], q_own.at[1], q_other.at[1], q_panel, sems.at[1])
-    attend_all(query, mine, theirs, key_pairs, value_pairs, attended, block)
+    attend_all(query, ones, mine, theirs, key_pairs, value_pairs, attended, block)
     finish(o_copies)
     finish(q_copies)
 
@@ -141,11 +156,11 @@
 
 
 def last_kernel(
-    narrow, hidden, query, mine, theirs, o_own, o_other, out,
+    narrow, hidden, query, ones, mine, theirs, o_own, o_other, out,
     o_panel, key_pairs, value_pairs, attended, result, sems, out_sems, *, block, chunk,
 ):
     copies = fetch(narrow[0], o_own.at[1], o_other.at[1], o_panel, sems)
-    attend_all(query, mine, theirs, key_pairs, value_pairs, attended, block)
+    attend_all(query, ones, mine, theirs, key_pairs, value_pairs, attended, block)
     finish(copies)
     leaving = []
     for step in range(hidden.shape[1] // chunk):
@@ -177,7 +192,7 @@
         attended = pltpu.VMEM((rows, width), jnp.bfloat16)
         pairs = [
             pltpu.VMEM((width // 128, 2 * count, 128), jnp.bfloat16),
-            pltpu.VMEM((width // 128, 2 * count, 256), jnp.bfloat16),
+            pltpu.VMEM((width // 128, 2 * count, 128), jnp.bfloat16),
         ]
         hidden_shape = jax.ShapeDtypeStruct((rows, width), jnp.bfloat16)
         dense = 2 * rows * width * width
@@ -189,14 +204,25 @@
                 flops=flops, bytes_accessed=4 * width * width, transcendentals=transcendentals
             )
 
+        gathered, ones = pl.pallas_call(
+            start_kernel,
+            out_shape=(
+                jax.ShapeDtypeStruct(latents.shape, jnp.bfloat16),
+                jax.ShapeDtypeStruct((2 * count, 128), jnp.bfloat16),
+            ),
+            in_specs=[VMEM],
+            out_specs=(VMEM, VMEM),
+            compiler_params=params,
+            cost_estimate=cost(8 * dense),
+        )(latents)
         q_other = swap(q_weight)
-        gathered = latents
+        o_other = swap(o_weight)
         step = wide // 2
         while step > 1:
-            received = lax.ppermute(gathered, "wide", [(i, i ^ step) for i in range(wide)])
+            source = latents if step == wide // 2 else gathered
+            received = lax.ppermute(source, "wide", [(i, i ^ step) for i in range(wide)])
             if step == wide // 2:
-                received, q_other, o_weight = after(received, q_other, o_weight)
-                o_other = swap(o_weight)
+                _, q_other = after(received, q_other)
                 normed, q_first = pl.pallas_call(
                     norm_kernel,
                     out_shape=(hidden_shape, jax.ShapeDtypeStruct((width // 2, width), jnp.bfloat16)),
@@ -204,7 +230,7 @@
                     out_specs=(VMEM, VMEM),
                     scratch_shapes=[pltpu.SemaphoreType.DMA],
                     compiler_params=params,
-                    cost_estimate=cost(dense),
+                    cost_estimate=cost(4 * dense),
                 )(queries, norm_gains, q_other)
             if step == 2:
                 received, normed = after(received, normed)
@@ -257,16 +283,16 @@
         hidden, query = pl.pallas_call(
             functools.partial(first_kernel, scale=scale, block=block, dense_block=rows),
             out_shape=(hidden_shape, hidden_shape),
-            in_specs=[SMEM] + [VMEM] * 5 + [ANY] * 4,
+            in_specs=[SMEM] + [VMEM] * 6 + [ANY] * 4,
             out_specs=(VMEM, VMEM),
             scratch_shapes=[panel, panel] + pairs + [attended, pltpu.SemaphoreType.DMA((2, 2))],
             compiler_params=params,
             cost_estimate=cost(2 * dense + attend_cost, rows * count * HEADS),
-        )(narrow, queries, query, first, first_other, norm_gains, q_weight, q_other, o_weight, o_other)
+        )(narrow, queries, query, ones, first, first_other, norm_gains, q_weight, q_other, o_weight, o_other)
         return pl.pallas_call(
             functools.partial(last_kernel, block=block, chunk=256),
             out_shape=hidden_shape,
-            in_specs=[SMEM] + [VMEM] * 4 + [ANY] * 2,
+            in_specs=[SMEM] + [VMEM] * 5 + [ANY] * 2,
             out_specs=ANY,
             scratch_shapes=[panel]
             + pairs
@@ -278,7 +304,7 @@
             ],
             compiler_params=params,
             cost_estimate=cost(attend_cost + dense, rows * count * HEADS),
-        )(narrow, hidden, query, second, second_other, o_weight, o_other)
+        )(narrow, hidden, query, ones, second, second_other, o_weight, o_other)
 
     return shards
 

time: 34.6 us -> 29.7 us (0.86)
  local copies, waits for them, and re-layouts: 5.6 us -> 0.75 us
  other arithmetic: 0.76 us -> 0.05 us
  Pallas kernels: 12.7 us -> 13.2 us
    unnamed x22 -> x16, local copies, waits for them, and re-layouts: 5.6 us -> 0.75 us
    concatenate x1, other arithmetic: 0.72 us -> 0.01 us  [shards(): gathered = jnp.concatenate([gathered, received], axis=0)]
    pallas_call x1, Pallas kernels: 0.76 us -> 1.38 us  [shards(): pl.pallas_call(norm_kernel, out_shape=(hidden_shape, jax.ShapeDtypeStruct...]
    pallas_call x1, Pallas kernels: 4.49 us -> 3.99 us  [shards(): pl.pallas_call(functools.partial(last_kernel, block=block, chunk=256), ou...]
    pallas_call x1, Pallas kernels: 5.41 us -> 5.79 us  [shards(): pl.pallas_call(functools.partial(first_kernel, scale=scale, block=block,...]
  transfers between devices with their start and end apart: 9 -> 9, of which waited for: 3 -> 4; matrix products, arithmetic and copies ran while one was open for 4% -> 0% of each run, Pallas kernels for 22% -> 29%
where the time goes in v2:
time: 29.7 us; the launch traced here: 29.4 us
  Pallas kernels  13.2 us (44%)
  starting transfers between devices  8.59 us (29%)
  waiting for transfers between devices  6.68 us (22%)
  local copies, waits for them, and re-layouts  0.75 us (3%)
    pallas_call x1, Pallas kernels, shards(): pl.pallas_call(functools.partial(first_kernel, scale=scale, block=block,...  5.79 us
    ppermute x2, starting transfers between devices, shards(): lax.ppermute(source, 'wide', [(i, i ^ step) for i in range(wide)])  5.57 us
    pallas_call x1, Pallas kernels, shards(): pl.pallas_call(functools.partial(last_kernel, block=block, chunk=256), ou...  3.99 us
    ppermute x4, waiting for transfers between devices, swap(): return lax.ppermute(array, 'narrow', [(0, 1), (1, 0)])  2.65 us
    ppermute x3, waiting for transfers between devices, shards(): lax.ppermute(array, ('wide', 'narrow'), [(i, i ^ mask) for i in devices])  2.42 us
    ppermute x3, starting transfers between devices, shards(): lax.ppermute(array, ('wide', 'narrow'), [(i, i ^ mask) for i in devices])  2.2 us
    ppermute x2, waiting for transfers between devices, shards(): lax.ppermute(source, 'wide', [(i, i ^ step) for i in range(wide)])  1.61 us
    pallas_call x1, Pallas kernels, shards(): pl.pallas_call(norm_kernel, out_shape=(hidden_shape, jax.ShapeDtypeStruct...  1.38 us
  transfers between devices with their start and end apart: 9, of which 4 were waited for; matrix products, arithmetic and copies ran while one was open for 0% of the time, Pallas kernels for 29%

profile of v2, /device:TPU:0, one launch (start us, length us, event | category | flops | bytes accessed | tf_op | source)
XLA Modules:
  0.0 29.4 jit_solution(3989730447330567103)
XLA Ops:
  0.0 0.5 %collective-permute-start.2 = (bf16[2,512,1024]{2,1,0:T(8,128)(2,1)}, bf16[2,512,1024]{2,1,0:T(8,128)(2,1)}, u32[]{:S(2)}, u32[]{:S(2)}) collective-permute-start(bf16[2,512,1024]{2,1,0:T(8,128)(2,1)} %q_own.3), channel_id=1, source_target_pairs={{0,1},{1,0},{2,3},{3,2},{4,5},{5,4},{6,7},{7,6},{8,9},{9,8},{10,11... | collective-permute-start | bytes 6291464 | tf_op jit(solution)/shard_map/ppermute | solution.py:178
  0.5 3.7 %collective-permute-start = (bf16[8,1024]{1,0:T(8,128)(2,1)}, bf16[8,1024]{1,0:T(8,128)(2,1)S(1)}, u32[]{:S(2)}, u32[]{:S(2)}) collective-permute-start(bf16[8,1024]{1,0:T(8,128)(2,1)} %latents.1), channel_id=1, source_target_pairs={{0,8},{2,10},{4,12},{6,14},{8,0},{10,2},{12,4},{14,6},{1,9},{3,11}... | collective-permute-start | bytes 49160 | tf_op jit(solution)/shard_map/ppermute | solution.py:223
  4.1 0.2 collective-permute-start.6
  4.3 0.7 %copy-done.6 = bf16[8,1024]{1,0:T(8,128)(2,1)S(1)} copy-done((bf16[8,1024]{1,0:T(8,128)(2,1)S(1)}, bf16[8,1024]{1,0:T(8,128)(2,1)}, u32[]{:S(2)}) %copy-start.6) | copy-done | bytes 16408
  5.0 1.0 %collective-permute-done = bf16[8,1024]{1,0:T(8,128)(2,1)S(1)} collective-permute-done((bf16[8,1024]{1,0:T(8,128)(2,1)}, bf16[8,1024]{1,0:T(8,128)(2,1)S(1)}, u32[]{:S(2)}, u32[]{:S(2)}) %collective-permute-start) | collective-permute-done | bytes 16416 | tf_op jit(solution)/shard_map/ppermute | solution.py:223
  6.1 1.9 %collective-permute-start.1 = (bf16[16,1024]{1,0:T(8,128)(2,1)S(1)}, bf16[16,1024]{1,0:T(8,128)(2,1)S(1)}, u32[]{:S(2)}, u32[]{:S(2)}) collective-permute-start(bf16[16,1024]{1,0:T(8,128)(2,1)S(1)} %pad_maximum_fusion.1), channel_id=1, source_target_pairs={{0,4},{2,6},{4,0},{6,2},{8,12},{10,14},{12,8},{14,10},{1,5},{3,7},... | collective-permute-start | bytes 98312 | tf_op jit(solution)/shard_map/ppermute | solution.py:223
  8.0 0.0 collective-permute-done.2.q_other
  8.0 1.4 %shard_map.74 = (bf16[512,1024]{1,0:T(8,128)(2,1)S(1)}, bf16[512,1024]{1,0:T(8,128)(2,1)S(1)}) custom-call(bf16[512,1024]{1,0:T(8,128)(2,1)S(1)} %copy-done.4, f32[2,1024]{1,0:T(2,128)S(1)} %copy-done.5, bf16[2,512,1024]{2,1,0:T(8,128)(2,1)} %collective-permute-done.2.q_other), custom_call_target="tpu_custom_call" | custom-call | flops 4294967296 | bytes 4194304 | tf_op jit(solution)/shard_map/pallas_call | solution.py:226
  9.4 0.6 %collective-permute-done.1 = bf16[16,1024]{1,0:T(8,128)(2,1)S(1)} collective-permute-done((bf16[16,1024]{1,0:T(8,128)(2,1)S(1)}, bf16[16,1024]{1,0:T(8,128)(2,1)S(1)}, u32[]{:S(2)}, u32[]{:S(2)}) %collective-permute-start.1) | collective-permute-done | bytes 32800 | tf_op jit(solution)/shard_map/ppermute | solution.py:223
  10.0 0.1 collective-permute-start.5
  10.1 1.9 %collective-permute-start.3 = (bf16[32,512]{1,0:T(8,128)(2,1)S(1)}, bf16[32,512]{1,0:T(8,128)(2,1)S(1)}, u32[]{:S(2)}, u32[]{:S(2)}) collective-permute-start(bf16[32,512]{1,0:T(8,128)(2,1)S(1)} %get-tuple-element.28), channel_id=1, source_target_pairs={{0,1},{1,0},{2,3},{3,2},{4,5},{5,4},{6,7},{7,6},{8,9},{9,8},{10,11... | collective-permute-start | bytes 98312 | tf_op jit(solution)/shard_map/ppermute | solution.py:247
  12.0 0.2 collective-permute-start.4
  12.2 1.3 %shard_map.75.query = bf16[512,1024]{1,0:T(8,128)(2,1)S(1)} custom-call(s32[1]{0:T(128)} %bitcast.narrow, bf16[512,1024]{1,0:T(8,128)(2,1)S(1)} %get-tuple-element.29.normed, bf16[2,512,1024]{2,1,0:T(8,128)(2,1)S(1)} %copy-done.1, bf16[512,1024]{1,0:T(8,128)(2,1)S(1)} %get-tuple-element.30.q_other), custom_call_target="tpu_custom_call" | custom-call | flops 1073741824 | bytes 4194304 | tf_op jit(solution)/shard_map/pallas_call | solution.py:260
  13.5 0.0 collective-permute-done.3
  13.5 2.4 %collective-permute-done.4 = bf16[32,512]{1,0:T(8,128)(2,1)S(1)} collective-permute-done((bf16[32,512]{1,0:T(8,128)(2,1)S(1)}, bf16[32,512]{1,0:T(8,128)(2,1)S(1)}, u32[]{:S(2)}, u32[]{:S(2)}) %collective-permute-start.4) | collective-permute-done | bytes 32800 | tf_op jit(solution)/shard_map/ppermute | solution.py:247
  15.9 0.0 copy-start
  15.9 0.0 collective-permute-done.6.o_other
  16.0 0.8 %shard_map.76 = (f32[2,128,1024]{2,1,0:T(8,128)S(1)}, f32[2,128,1024]{2,1,0:T(8,128)S(1)}) custom-call(bf16[128,512]{1,0:T(8,128)(2,1)S(1)} %pad_maximum_fusion.latents, bf16[2,512,1024]{2,1,0:T(8,128)(2,1)S(1)} %copy-done.2, bf16[2,512,1024]{2,1,0:T(8,128)(2,1)S(1)} %copy-done.3), custom_call_target="tpu_custom_call" | custom-call | flops 536870912 | bytes 4194304 | tf_op jit(solution)/shard_map/pallas_call | solution.py:271
  16.7 0.1 collective-permute-start.7
  16.8 2.6 %collective-permute-done.7.theirs = f32[2,128,1024]{2,1,0:T(8,128)S(1)} collective-permute-done((f32[2,128,1024]{2,1,0:T(8,128)S(1)}, f32[2,128,1024]{2,1,0:T(8,128)S(1)}, u32[]{:S(2)}, u32[]{:S(2)}) %collective-permute-start.7) | collective-permute-done | bytes 1048608 | tf_op jit(solution)/shard_map/ppermute | solution.py:178
  19.5 0.1 collective-permute-start.8
  19.6 5.8 %shard_map.77 = (bf16[512,1024]{1,0:T(8,128)(2,1)S(1)}, bf16[512,1024]{1,0:T(8,128)(2,1)S(1)}) custom-call(s32[1]{0:T(128)} %bitcast.narrow, bf16[512,1024]{1,0:T(8,128)(2,1)S(1)} %copy-done.4, bf16[512,1024]{1,0:T(8,128)(2,1)S(1)} %shard_map.75.query, bf16[256,128]{1,0:T(8,128)(2,1)S(1)} %get-tuple-element.32.ones, ...), custom_call_target="tpu_custom_call" | custom-call | flops 2684354560 | bytes 4194304 | tf_op jit(solution)/shard_map/pallas_call | solution.py:283
  25.4 0.0 collective-permute-done.8.theirs
  25.4 4.0 %shard_map.78 = bf16[512,1024]{1,0:T(8,128)(2,1)} custom-call(s32[1]{0:T(128)} %bitcast.narrow, bf16[512,1024]{1,0:T(8,128)(2,1)S(1)} %get-tuple-element.38.hidden, bf16[512,1024]{1,0:T(8,128)(2,1)S(1)} %get-tuple-element.39.query, bf16[256,128]{1,0:T(8,128)(2,1)S(1)} %get-tuple-element.32.ones, f32[2,128,1024]{2,1,0:T(8,128)S(1)} %get-tuple-element.40.mine, ...), custom_call_target="tpu_custom_call" | custom-call | flops 1610612736 | bytes 4194304 | tf_op jit(solution)/shard_map/pallas_call | solution.py:292
  (22 shorter events, 0.1 us)
Async XLA Ops:
  0.0 8.0 %copy-start.5 = (f32[2,1024]{1,0:T(2,128)S(1)}, f32[2,1024]{1,0:T(2,128)}, u32[]{:S(2)}) copy-start(f32[2,1024]{1,0:T(2,128)} %gains.3) | copy-start | bytes 24580
  0.0 8.0 %copy-start.4 = (bf16[512,1024]{1,0:T(8,128)(2,1)S(1)}, bf16[512,1024]{1,0:T(8,128)(2,1)}, u32[]{:S(2)}) copy-start(bf16[512,1024]{1,0:T(8,128)(2,1)} %hidden.3) | copy-start | bytes 3145732
  0.0 8.0 %collective-permute-start.2 = (bf16[2,512,1024]{2,1,0:T(8,128)(2,1)}, bf16[2,512,1024]{2,1,0:T(8,128)(2,1)}, u32[]{:S(2)}, u32[]{:S(2)}) collective-permute-start(bf16[2,512,1024]{2,1,0:T(8,128)(2,1)} %q_own.3), channel_id=1, source_target_pairs={{0,1},{1,0},{2,3},{3,2},{4,5},{5,4},{6,7},{7,6},{8,9},{9,8},{10,11... | collective-permute-start | bytes 6291464 | tf_op jit(solution)/shard_map/ppermute | solution.py:178
  0.5 5.6 %collective-permute-start = (bf16[8,1024]{1,0:T(8,128)(2,1)}, bf16[8,1024]{1,0:T(8,128)(2,1)S(1)}, u32[]{:S(2)}, u32[]{:S(2)}) collective-permute-start(bf16[8,1024]{1,0:T(8,128)(2,1)} %latents.1), channel_id=1, source_target_pairs={{0,8},{2,10},{4,12},{6,14},{8,0},{10,2},{12,4},{14,6},{1,9},{3,11}... | collective-permute-start | bytes 49160 | tf_op jit(solution)/shard_map/ppermute | solution.py:223
  4.1 11.8 %collective-permute-start.6 = (bf16[2,512,1024]{2,1,0:T(8,128)(2,1)}, bf16[2,512,1024]{2,1,0:T(8,128)(2,1)S(1)}, u32[]{:S(2)}, u32[]{:S(2)}) collective-permute-start(bf16[2,512,1024]{2,1,0:T(8,128)(2,1)} %o_own.3), channel_id=1, source_target_pairs={{0,1},{1,0},{2,3},{3,2},{4,5},{5,4},{6,7},{7,6},{8,9},{9,8},{10,11... | collective-permute-start | bytes 6291464 | tf_op jit(solution)/shard_map/ppermute | solution.py:178
  4.3 0.7 %copy-start.6 = (bf16[8,1024]{1,0:T(8,128)(2,1)S(1)}, bf16[8,1024]{1,0:T(8,128)(2,1)}, u32[]{:S(2)}) copy-start(bf16[8,1024]{1,0:T(8,128)(2,1)} %latents.1) | copy-start | bytes 49156
  6.1 3.9 %collective-permute-start.1 = (bf16[16,1024]{1,0:T(8,128)(2,1)S(1)}, bf16[16,1024]{1,0:T(8,128)(2,1)S(1)}, u32[]{:S(2)}, u32[]{:S(2)}) collective-permute-start(bf16[16,1024]{1,0:T(8,128)(2,1)S(1)} %pad_maximum_fusion.1), channel_id=1, source_target_pairs={{0,4},{2,6},{4,0},{6,2},{8,12},{10,14},{12,8},{14,10},{1,5},{3,7},... | collective-permute-start | bytes 98312 | tf_op jit(solution)/shard_map/ppermute | solution.py:223
  8.0 4.2 %copy-start.1 = (bf16[2,512,1024]{2,1,0:T(8,128)(2,1)S(1)}, bf16[2,512,1024]{2,1,0:T(8,128)(2,1)}, u32[]{:S(2)}) copy-start(bf16[2,512,1024]{2,1,0:T(8,128)(2,1)} %q_own.3) | copy-start | bytes 6291460
  10.0 5.9 %collective-permute-start.5 = (bf16[32,512]{1,0:T(8,128)(2,1)S(1)}, bf16[32,512]{1,0:T(8,128)(2,1)S(1)}, u32[]{:S(2)}, u32[]{:S(2)}) collective-permute-start(bf16[32,512]{1,0:T(8,128)(2,1)S(1)} %get-tuple-element.28), channel_id=1, source_target_pairs={{0,3},{1,2},{2,1},{3,0},{4,7},{5,6},{6,5},{7,4},{8,11},{9,10},{10,... | collective-permute-start | bytes 98312 | tf_op jit(solution)/shard_map/ppermute | solution.py:247
  10.1 3.4 %collective-permute-start.3 = (bf16[32,512]{1,0:T(8,128)(2,1)S(1)}, bf16[32,512]{1,0:T(8,128)(2,1)S(1)}, u32[]{:S(2)}, u32[]{:S(2)}) collective-permute-start(bf16[32,512]{1,0:T(8,128)(2,1)S(1)} %get-tuple-element.28), channel_id=1, source_target_pairs={{0,1},{1,0},{2,3},{3,2},{4,5},{5,4},{6,7},{7,6},{8,9},{9,8},{10,11... | collective-permute-start | bytes 98312 | tf_op jit(solution)/shard_map/ppermute | solution.py:247
  12.0 3.9 %collective-permute-start.4 = (bf16[32,512]{1,0:T(8,128)(2,1)S(1)}, bf16[32,512]{1,0:T(8,128)(2,1)S(1)}, u32[]{:S(2)}, u32[]{:S(2)}) collective-permute-start(bf16[32,512]{1,0:T(8,128)(2,1)S(1)} %get-tuple-element.27), channel_id=1, source_target_pairs={{0,2},{1,3},{2,0},{3,1},{4,6},{5,7},{6,4},{7,5},{8,10},{9,11},{10,... | collective-permute-start | bytes 98312 | tf_op jit(solution)/shard_map/ppermute | solution.py:247
  12.2 3.8 %copy-start.2 = (bf16[2,512,1024]{2,1,0:T(8,128)(2,1)S(1)}, bf16[2,512,1024]{2,1,0:T(8,128)(2,1)}, u32[]{:S(2)}) copy-start(bf16[2,512,1024]{2,1,0:T(8,128)(2,1)} %k_own.1) | copy-start | bytes 6291460
  12.2 3.8 %copy-start.3 = (bf16[2,512,1024]{2,1,0:T(8,128)(2,1)S(1)}, bf16[2,512,1024]{2,1,0:T(8,128)(2,1)}, u32[]{:S(2)}) copy-start(bf16[2,512,1024]{2,1,0:T(8,128)(2,1)} %v_own.1) | copy-start | bytes 6291460
  15.9 3.7 %copy-start = (bf16[2,512,1024]{2,1,0:T(8,128)(2,1)S(1)}, bf16[2,512,1024]{2,1,0:T(8,128)(2,1)}, u32[]{:S(2)}) copy-start(bf16[2,512,1024]{2,1,0:T(8,128)(2,1)} %o_own.3) | copy-start | bytes 6291460
  16.7 2.7 %collective-permute-start.7 = (f32[2,128,1024]{2,1,0:T(8,128)S(1)}, f32[2,128,1024]{2,1,0:T(8,128)S(1)}, u32[]{:S(2)}, u32[]{:S(2)}) collective-permute-start(f32[2,128,1024]{2,1,0:T(8,128)S(1)} %get-tuple-element.34.mine), channel_id=1, source_target_pairs={{0,1},{1,0},{2,3},{3,2},{4,5},{5,4},{6,7},{7,6},{8,9},{9,8},{10,11... | collective-permute-start | bytes 3145736 | tf_op jit(solution)/shard_map/ppermute | solution.py:178
  19.5 5.9 %collective-permute-start.8 = (f32[2,128,1024]{2,1,0:T(8,128)S(1)}, f32[2,128,1024]{2,1,0:T(8,128)S(1)}, u32[]{:S(2)}, u32[]{:S(2)}) collective-permute-start(f32[2,128,1024]{2,1,0:T(8,128)S(1)} %get-tuple-element.40.mine), channel_id=1, source_target_pairs={{0,1},{1,0},{2,3},{3,2},{4,5},{5,4},{6,7},{7,6},{8,9},{9,8},{10,11... | collective-permute-start | bytes 3145736 | tf_op jit(solution)/shard_map/ppermute | solution.py:178

commit v3 on v2

--- a/solution.py
+++ b/solution.py
@@ -73,12 +73,16 @@
     copy.wait()
 
 
-def query_kernel(narrow, normed, q_own, q_other, out, *, scale, block):
-    @pl.loop(0, normed.shape[0] // block)
-    def _(step):
-        rows = pl.ds(pl.multiple_of(step * block, block), block)
-        query = split_dot(narrow[0], normed.at[rows, :], q_own.at[0], q_other)
-        out[rows, :] = (query * scale).astype(jnp.bfloat16)
+def query_kernel(narrow, normed, q_own, q_other, o_own, out, o_first, o_second, sems, *, scale):
+    copies = [
+        pltpu.make_async_copy(o_own.at[layer], target, sems.at[layer])
+        for layer, target in enumerate((o_first, o_second))
+    ]
+    for copy in copies:
+        copy.start()
+    query = split_dot(narrow[0], normed, q_own.at[0], q_other)
+    out[...] = (query * scale).astype(jnp.bfloat16)
+    finish(copies)
 
 
 def latent_kernel(latents, k_own, v_own, first, second):
@@ -136,30 +140,34 @@
         pl.loop(0, steps)(one_block)
 
 
-def first_kernel(
-    narrow, hidden, query, ones, mine, theirs, gains, q_own, q_other, o_own, o_other, out, next_query,
-    q_panel, o_panel, key_pairs, value_pairs, attended, sems, *, scale, block, dense_block,
+def first_kernel(query, ones, mine, theirs, out, key_pairs, value_pairs, *, block):
+    attend_all(query, ones, mine, theirs, key_pairs, value_pairs, out, block)
+
+
+def between_kernel(
+    narrow, hidden, attended, gains, o_own, o_other, q_own, q_other, out, next_query,
+    q_panel, o_half, sums, sems, o_sem, *, scale,
 ):
-    o_copies = fetch(narrow[0], o_own.at[0], o_other.at[0], o_panel, sems.at[0])
-    q_copies = fetch(narrow[0], q_own.at[1], q_other.at[1], q_panel, sems.at[1])
-    attend_all(query, ones, mine, theirs, key_pairs, value_pairs, attended, block)
-    finish(o_copies)
+    o_copy = pltpu.make_async_copy(o_other, o_half, o_sem)
+    o_copy.start()
+    q_copies = fetch(narrow[0], q_own.at[1], q_other.at[1], q_panel, sems)
+    half = o_half.shape[0]
+    mine = attended[:, pl.ds(pl.multiple_of(narrow[0] * half, half), half)]
+    theirs = attended[:, pl.ds(pl.multiple_of((1 - narrow[0]) * half, half), half)]
+    sums[...] = hidden[...].astype(jnp.float32) + dot(mine, o_own[...])
+    o_copy.wait()
+    state = (sums[...] + dot(theirs, o_half[...])).astype(jnp.bfloat16)
+    out[...] = state
+    normed = layer_norm(state, gains[1:2, :])
     finish(q_copies)
-
-    @pl.loop(0, hidden.shape[0] // dense_block)
-    def _(step):
-        rows = pl.ds(pl.multiple_of(step * dense_block, dense_block), dense_block)
-        state = add_output(hidden[rows, :], attended[rows, :], o_panel[...])
-        out[rows, :] = state
-        normed = layer_norm(state, gains[1:2, :])
-        next_query[rows, :] = (dot(normed, q_panel[...]) * scale).astype(jnp.bfloat16)
+    next_query[...] = (dot(normed, q_panel[...]) * scale).astype(jnp.bfloat16)
 
 
 def last_kernel(
     narrow, hidden, query, ones, mine, theirs, o_own, o_other, out,
     o_panel, key_pairs, value_pairs, attended, result, sems, out_sems, *, block, chunk,
 ):
-    copies = fetch(narrow[0], o_own.at[1], o_other.at[1], o_panel, sems)
+    copies = fetch(narrow[0], o_own, o_other, o_panel, sems)
     attend_all(query, ones, mine, theirs, key_pairs, value_pairs, attended, block)
     finish(copies)
     leaving = []
@@ -189,7 +197,7 @@
         block = min(256, max(16, 32768 // count))
         params = pltpu.CompilerParams(vmem_limit_bytes=GRANT if count <= 256 else LARGE_GRANT)
         panel = pltpu.VMEM((width, width), jnp.bfloat16)
-        attended = pltpu.VMEM((rows, width), jnp.bfloat16)
+        row_scratch = pltpu.VMEM((rows, width), jnp.bfloat16)
         pairs = [
             pltpu.VMEM((width // 128, 2 * count, 128), jnp.bfloat16),
             pltpu.VMEM((width // 128, 2 * count, 128), jnp.bfloat16),
@@ -216,7 +224,6 @@
             cost_estimate=cost(8 * dense),
         )(latents)
         q_other = swap(q_weight)
-        o_other = swap(o_weight)
         step = wide // 2
         while step > 1:
             source = latents if step == wide // 2 else gathered
@@ -257,15 +264,17 @@
             axis=0,
         )
 
-        query = pl.pallas_call(
-            functools.partial(query_kernel, scale=scale, block=rows),
-            out_shape=hidden_shape,
-            in_specs=[SMEM] + [VMEM] * 3,
-            out_specs=VMEM,
+        half_shape = jax.ShapeDtypeStruct((half, width), jnp.bfloat16)
+        query, o_first, o_second = pl.pallas_call(
+            functools.partial(query_kernel, scale=scale),
+            out_shape=(hidden_shape, half_shape, half_shape),
+            in_specs=[SMEM] + [VMEM] * 3 + [ANY],
+            out_specs=(VMEM, VMEM, VMEM),
+            scratch_shapes=[pltpu.SemaphoreType.DMA((2,))],
             compiler_params=params,
             cost_estimate=cost(dense),
-        )(narrow, normed, q_weight, q_first)
-        gathered, query, o_other = after(gathered, query, o_other)
+        )(narrow, normed, q_weight, q_first, o_weight)
+        gathered, query = after(gathered, query)
 
         partial_shape = jax.ShapeDtypeStruct((2, count, width), jnp.float32)
         first, second = pl.pallas_call(
@@ -277,18 +286,36 @@
             cost_estimate=cost(latent_cost),
         )(gathered, k_weight, v_weight)
         first_other = swap(first)
-        first_other, second = after(first_other, second)
+        first_other, o_sent = after(first_other, o_first)
+        o_other = swap(o_sent)
+
+        attended = pl.pallas_call(
+            functools.partial(first_kernel, block=block),
+            out_shape=hidden_shape,
+            in_specs=[VMEM] * 4,
+            out_specs=VMEM,
+            scratch_shapes=pairs,
+            compiler_params=params,
+            cost_estimate=cost(2 * attend_cost, rows * count * HEADS),
+        )(query, ones, first, first_other)
+        attended, o_other, second, o_sent = after(attended, o_other, second, o_second)
         second_other = swap(second)
-
+        o_last = swap(o_sent)
         hidden, query = pl.pallas_call(
-            functools.partial(first_kernel, scale=scale, block=block, dense_block=rows),
+            functools.partial(between_kernel, scale=scale),
             out_shape=(hidden_shape, hidden_shape),
-            in_specs=[SMEM] + [VMEM] * 6 + [ANY] * 4,
+            in_specs=[SMEM] + [VMEM] * 4 + [ANY] * 3,
             out_specs=(VMEM, VMEM),
-            scratch_shapes=[panel, panel] + pairs + [attended, pltpu.SemaphoreType.DMA((2, 2))],
-            compiler_params=params,
-            cost_estimate=cost(2 * dense + attend_cost, rows * count * HEADS),
-        )(narrow, queries, query, ones, first, first_other, norm_gains, q_weight, q_other, o_weight, o_other)
+            scratch_shapes=[
+                panel,
+                pltpu.VMEM((half, width), jnp.bfloat16),
+                pltpu.VMEM((rows, width), jnp.float32),
+                pltpu.SemaphoreType.DMA((2,)),
+                pltpu.SemaphoreType.DMA,
+            ],
+            compiler_params=params,
+            cost_estimate=cost(2 * dense),
+        )(narrow, queries, attended, norm_gains, o_first, o_other, q_weight, q_other)
         return pl.pallas_call(
             functools.partial(last_kernel, block=block, chunk=256),
             out_shape=hidden_shape,
@@ -297,14 +324,14 @@
             scratch_shapes=[panel]
             + pairs
             + [
-                attended,
-                pltpu.VMEM((rows, width), jnp.bfloat16),
+                row_scratch,
+                row_scratch,
                 pltpu.SemaphoreType.DMA((2,)),
                 pltpu.SemaphoreType.DMA((width // 256,)),
             ],
             compiler_params=params,
             cost_estimate=cost(attend_cost + dense, rows * count * HEADS),
-        )(narrow, hidden, query, ones, second, second_other, o_weight, o_other)
+        )(narrow, hidden, query, ones, second, second_other, o_second, o_last)
 
     return shards
 

time: 29.7 us -> 30.5 us (1.027)
  waiting for transfers between devices: 6.68 us -> 8.21 us
  Pallas kernels: 13.2 us -> 12.1 us
  starting transfers between devices: 8.59 us -> 8.94 us
    ppermute x4 -> x5, waiting for transfers between devices: 2.65 us -> 3.64 us  [swap(): return lax.ppermute(array, 'narrow', [(0, 1), (1, 0)])]
    ppermute x2, waiting for transfers between devices: 1.61 us -> 2.35 us  [shards(): lax.ppermute(source, 'wide', [(i, i ^ step) for i in range(wide)])]
    pallas_call x1, Pallas kernels: 1.38 us -> 0.76 us  [shards(): pl.pallas_call(norm_kernel, out_shape=(hidden_shape, jax.ShapeDtypeStruct...]
    pallas_call x2 -> x3, Pallas kernels: 7.05 us -> 6.6 us  [the longest x1 3.48 us: shards(): pl.pallas_call(functools.partial(between_kernel, scale=scale), out_shape=...]
    ppermute x4 -> x5, starting transfers between devices: 0.83 us -> 1.17 us  [swap(): return lax.ppermute(array, 'narrow', [(0, 1), (1, 0)])]
  transfers between devices with their start and end apart: 9 -> 10, of which waited for: 4 -> 6; matrix products, arithmetic and copies ran while one was open for 0% -> 0% of each run, Pallas kernels for 29% -> 24%
where the time goes in v3:
time: 30.5 us; the launch traced here: 30.2 us
  Pallas kernels  12.1 us (40%)
  starting transfers between devices  8.94 us (29%)
  waiting for transfers between devices  8.21 us (27%)
  local copies, waits for them, and re-layouts  0.78 us (3%)
    ppermute x2, starting transfers between devices, shards(): lax.ppermute(source, 'wide', [(i, i ^ step) for i in range(wide)])  5.57 us
    pallas_call x1, Pallas kernels, shards(): pl.pallas_call(functools.partial(last_kernel, block=block, chunk=256), ou...  3.98 us
    ppermute x5, waiting for transfers between devices, swap(): return lax.ppermute(array, 'narrow', [(0, 1), (1, 0)])  3.64 us
    pallas_call x1, Pallas kernels, shards(): pl.pallas_call(functools.partial(between_kernel, scale=scale), out_shape=...  3.48 us
    ppermute x2, waiting for transfers between devices, shards(): lax.ppermute(source, 'wide', [(i, i ^ step) for i in range(wide)])  2.35 us
    ppermute x3, waiting for transfers between devices, shards(): lax.ppermute(array, ('wide', 'narrow'), [(i, i ^ mask) for i in devices])  2.22 us
    ppermute x3, starting transfers between devices, shards(): lax.ppermute(array, ('wide', 'narrow'), [(i, i ^ mask) for i in devices])  2.2 us
    pallas_call x1, Pallas kernels, shards(): pl.pallas_call(functools.partial(first_kernel, block=block), out_shape=hi...  1.68 us
  transfers between devices with their start and end apart: 10, of which 6 were waited for; matrix products, arithmetic and copies ran while one was open for 0% of the time, Pallas kernels for 24%

profile of v3, /device:TPU:0, one launch (start us, length us, event | category | flops | bytes accessed | tf_op | source)
XLA Modules:
  0.0 30.2 jit_solution(6844962177720773304)
XLA Ops:
  0.0 0.5 %collective-permute-start.2 = (bf16[2,512,1024]{2,1,0:T(8,128)(2,1)}, bf16[2,512,1024]{2,1,0:T(8,128)(2,1)S(1)}, u32[]{:S(2)}, u32[]{:S(2)}) collective-permute-start(bf16[2,512,1024]{2,1,0:T(8,128)(2,1)} %q_own.3), channel_id=1, source_target_pairs={{0,1},{1,0},{2,3},{3,2},{4,5},{5,4},{6,7},{7,6},{8,9},{9,8},{10,11... | collective-permute-start | bytes 6291464 | tf_op jit(solution)/shard_map/ppermute | solution.py:186
  0.5 3.7 %collective-permute-start = (bf16[8,1024]{1,0:T(8,128)(2,1)}, bf16[8,1024]{1,0:T(8,128)(2,1)S(1)}, u32[]{:S(2)}, u32[]{:S(2)}) collective-permute-start(bf16[8,1024]{1,0:T(8,128)(2,1)} %latents.1), channel_id=1, source_target_pairs={{0,8},{2,10},{4,12},{6,14},{8,0},{10,2},{12,4},{14,6},{1,9},{3,11}... | collective-permute-start | bytes 49160 | tf_op jit(solution)/shard_map/ppermute | solution.py:230
  4.1 0.7 %copy-done.6 = bf16[8,1024]{1,0:T(8,128)(2,1)S(1)} copy-done((bf16[8,1024]{1,0:T(8,128)(2,1)S(1)}, bf16[8,1024]{1,0:T(8,128)(2,1)}, u32[]{:S(2)}) %copy-start.6) | copy-done | bytes 16408
  4.9 1.1 %collective-permute-done = bf16[8,1024]{1,0:T(8,128)(2,1)S(1)} collective-permute-done((bf16[8,1024]{1,0:T(8,128)(2,1)}, bf16[8,1024]{1,0:T(8,128)(2,1)S(1)}, u32[]{:S(2)}, u32[]{:S(2)}) %collective-permute-start) | collective-permute-done | bytes 16416 | tf_op jit(solution)/shard_map/ppermute | solution.py:230
  6.1 1.9 %collective-permute-start.1 = (bf16[16,1024]{1,0:T(8,128)(2,1)S(1)}, bf16[16,1024]{1,0:T(8,128)(2,1)S(1)}, u32[]{:S(2)}, u32[]{:S(2)}) collective-permute-start(bf16[16,1024]{1,0:T(8,128)(2,1)S(1)} %pad_maximum_fusion.1), channel_id=1, source_target_pairs={{0,4},{2,6},{4,0},{6,2},{8,12},{10,14},{12,8},{14,10},{1,5},{3,7},... | collective-permute-start | bytes 98312 | tf_op jit(solution)/shard_map/ppermute | solution.py:230
  8.0 0.8 %shard_map.74 = (bf16[512,1024]{1,0:T(8,128)(2,1)S(1)}, bf16[512,1024]{1,0:T(8,128)(2,1)S(1)}) custom-call(bf16[512,1024]{1,0:T(8,128)(2,1)S(1)} %copy-done.4, f32[2,1024]{1,0:T(2,128)S(1)} %copy-done.5, bf16[2,512,1024]{2,1,0:T(8,128)(2,1)S(1)} %collective-permute-done.2.q_other), custom_call_target="tpu_custom_call" | custom-call | flops 4294967296 | bytes 4194304 | tf_op jit(solution)/shard_map/pallas_call | solution.py:233
  8.8 1.2 %collective-permute-done.1 = bf16[16,1024]{1,0:T(8,128)(2,1)S(1)} collective-permute-done((bf16[16,1024]{1,0:T(8,128)(2,1)S(1)}, bf16[16,1024]{1,0:T(8,128)(2,1)S(1)}, u32[]{:S(2)}, u32[]{:S(2)}) %collective-permute-start.1) | collective-permute-done | bytes 32800 | tf_op jit(solution)/shard_map/ppermute | solution.py:230
  10.0 0.1 collective-permute-start.5
  10.1 1.9 %collective-permute-start.3 = (bf16[32,512]{1,0:T(8,128)(2,1)S(1)}, bf16[32,512]{1,0:T(8,128)(2,1)S(1)}, u32[]{:S(2)}, u32[]{:S(2)}) collective-permute-start(bf16[32,512]{1,0:T(8,128)(2,1)S(1)} %get-tuple-element.34), channel_id=1, source_target_pairs={{0,1},{1,0},{2,3},{3,2},{4,5},{5,4},{6,7},{7,6},{8,9},{9,8},{10,11... | collective-permute-start | bytes 98312 | tf_op jit(solution)/shard_map/ppermute | solution.py:254
  12.0 0.2 collective-permute-start.4
  12.2 1.4 %shard_map.75 = (bf16[512,1024]{1,0:T(8,128)(2,1)S(1)}, bf16[512,1024]{1,0:T(8,128)(2,1)S(1)}, bf16[512,1024]{1,0:T(8,128)(2,1)S(1)}) custom-call(s32[1]{0:T(128)} %bitcast.narrow, bf16[512,1024]{1,0:T(8,128)(2,1)S(1)} %get-tuple-element.35.normed, bf16[2,512,1024]{2,1,0:T(8,128)(2,1)S(1)} %copy-done, bf16[512,1024]{1,0:T(8,128)(2,1)S(1)} %get-tuple-element.36.q_other, ...), custom_call_target="tpu_custom_call" | custom-call | flops 1073741824 | bytes 4194304 | tf_op jit(solution)/shard_map/pallas_call | solution.py:268
  13.7 2.2 %collective-permute-done.4 = bf16[32,512]{1,0:T(8,128)(2,1)S(1)} collective-permute-done((bf16[32,512]{1,0:T(8,128)(2,1)S(1)}, bf16[32,512]{1,0:T(8,128)(2,1)S(1)}, u32[]{:S(2)}, u32[]{:S(2)}) %collective-permute-start.4) | collective-permute-done | bytes 32800 | tf_op jit(solution)/shard_map/ppermute | solution.py:254
  15.9 0.0 collective-permute-done.5
  16.0 0.7 %shard_map.76 = (f32[2,128,1024]{2,1,0:T(8,128)S(1)}, f32[2,128,1024]{2,1,0:T(8,128)S(1)}) custom-call(bf16[128,512]{1,0:T(8,128)(2,1)S(1)} %pad_maximum_fusion.latents, bf16[2,512,1024]{2,1,0:T(8,128)(2,1)S(1)} %copy-done.2, bf16[2,512,1024]{2,1,0:T(8,128)(2,1)S(1)} %copy-done.3), custom_call_target="tpu_custom_call" | custom-call | flops 536870912 | bytes 4194304 | tf_op jit(solution)/shard_map/pallas_call | solution.py:280
  16.7 0.1 collective-permute-start.6
  16.8 2.6 %collective-permute-done.6.theirs = f32[2,128,1024]{2,1,0:T(8,128)S(1)} collective-permute-done((f32[2,128,1024]{2,1,0:T(8,128)S(1)}, f32[2,128,1024]{2,1,0:T(8,128)S(1)}, u32[]{:S(2)}, u32[]{:S(2)}) %collective-permute-start.6) | collective-permute-done | bytes 1048608 | tf_op jit(solution)/shard_map/ppermute | solution.py:186
  19.4 0.1 collective-permute-start.7
  19.6 1.7 %shard_map.77.attended = bf16[512,1024]{1,0:T(8,128)(2,1)S(1)} custom-call(bf16[512,1024]{1,0:T(8,128)(2,1)S(1)} %get-tuple-element.38.query, bf16[256,128]{1,0:T(8,128)(2,1)S(1)} %get-tuple-element.39.ones, f32[2,128,1024]{2,1,0:T(8,128)S(1)} %get-tuple-element.41.mine, f32[2,128,1024]{2,1,0:T(8,128)S(1)} %collective-permute-done.6.theirs), custom_call_target="tpu_custom_call" | custom-call | flops 1073741824 | bytes 4194304 | tf_op jit(solution)/shard_map/pallas_call | solution.py:292
  21.2 0.8 %collective-permute-done.7.o_other = bf16[512,1024]{1,0:T(8,128)(2,1)S(1)} collective-permute-done((bf16[512,1024]{1,0:T(8,128)(2,1)S(1)}, bf16[512,1024]{1,0:T(8,128)(2,1)S(1)}, u32[]{:S(2)}, u32[]{:S(2)}) %collective-permute-start.7) | collective-permute-done | bytes 1048608 | tf_op jit(solution)/shard_map/ppermute | solution.py:186
  22.1 0.1 collective-permute-start.9
  22.2 0.4 %collective-permute-start.8 = (f32[2,128,1024]{2,1,0:T(8,128)S(1)}, f32[2,128,1024]{2,1,0:T(8,128)S(1)}, u32[]{:S(2)}, u32[]{:S(2)}) collective-permute-start(f32[2,128,1024]{2,1,0:T(8,128)S(1)} %get-tuple-element.51.mine), channel_id=1, source_target_pairs={{0,1},{1,0},{2,3},{3,2},{4,5},{5,4},{6,7},{7,6},{8,9},{9,8},{10,11... | collective-permute-start | bytes 3145736 | tf_op jit(solution)/shard_map/ppermute | solution.py:186
  22.6 3.5 %shard_map.78 = (bf16[512,1024]{1,0:T(8,128)(2,1)S(1)}, bf16[512,1024]{1,0:T(8,128)(2,1)S(1)}) custom-call(s32[1]{0:T(128)} %bitcast.narrow, bf16[512,1024]{1,0:T(8,128)(2,1)S(1)} %copy-done.4, bf16[512,1024]{1,0:T(8,128)(2,1)S(1)} %shard_map.77.attended, f32[2,1024]{1,0:T(2,128)S(1)} %copy-done.5, bf16[512,1024]{1,0:T(8,128)(2,1)S(1)} %get-tuple-element.44.o_own, ...), custom_call_target="tpu_custom_call" | custom-call | flops 2147483648 | bytes 4194304 | tf_op jit(solution)/shard_map/pallas_call | solution.py:304
  26.1 0.1 collective-permute-done.8.theirs
  26.2 4.0 %shard_map.79 = bf16[512,1024]{1,0:T(8,128)(2,1)} custom-call(s32[1]{0:T(128)} %bitcast.narrow, bf16[512,1024]{1,0:T(8,128)(2,1)S(1)} %get-tuple-element.49.hidden, bf16[512,1024]{1,0:T(8,128)(2,1)S(1)} %get-tuple-element.50.query, bf16[256,128]{1,0:T(8,128)(2,1)S(1)} %get-tuple-element.39.ones, f32[2,128,1024]{2,1,0:T(8,128)S(1)} %get-tuple-element.51.mine, ...), custom_call_target="tpu_custom_call" | custom-call | flops 1610612736 | bytes 4194304 | tf_op jit(solution)/shard_map/pallas_call | solution.py:319
  (25 shorter events, 0.1 us)
Async XLA Ops:
  0.0 8.0 %copy-start.5 = (f32[2,1024]{1,0:T(2,128)S(1)}, f32[2,1024]{1,0:T(2,128)}, u32[]{:S(2)}) copy-start(f32[2,1024]{1,0:T(2,128)} %gains.3) | copy-start | bytes 24580
  0.0 8.0 %copy-start.4 = (bf16[512,1024]{1,0:T(8,128)(2,1)S(1)}, bf16[512,1024]{1,0:T(8,128)(2,1)}, u32[]{:S(2)}) copy-start(bf16[512,1024]{1,0:T(8,128)(2,1)} %hidden.3) | copy-start | bytes 3145732
  0.0 8.0 %collective-permute-start.2 = (bf16[2,512,1024]{2,1,0:T(8,128)(2,1)}, bf16[2,512,1024]{2,1,0:T(8,128)(2,1)S(1)}, u32[]{:S(2)}, u32[]{:S(2)}) collective-permute-start(bf16[2,512,1024]{2,1,0:T(8,128)(2,1)} %q_own.3), channel_id=1, source_target_pairs={{0,1},{1,0},{2,3},{3,2},{4,5},{5,4},{6,7},{7,6},{8,9},{9,8},{10,11... | collective-permute-start | bytes 6291464 | tf_op jit(solution)/shard_map/ppermute | solution.py:186
  0.5 5.6 %collective-permute-start = (bf16[8,1024]{1,0:T(8,128)(2,1)}, bf16[8,1024]{1,0:T(8,128)(2,1)S(1)}, u32[]{:S(2)}, u32[]{:S(2)}) collective-permute-start(bf16[8,1024]{1,0:T(8,128)(2,1)} %latents.1), channel_id=1, source_target_pairs={{0,8},{2,10},{4,12},{6,14},{8,0},{10,2},{12,4},{14,6},{1,9},{3,11}... | collective-permute-start | bytes 49160 | tf_op jit(solution)/shard_map/ppermute | solution.py:230
  4.1 0.8 %copy-start.6 = (bf16[8,1024]{1,0:T(8,128)(2,1)S(1)}, bf16[8,1024]{1,0:T(8,128)(2,1)}, u32[]{:S(2)}) copy-start(bf16[8,1024]{1,0:T(8,128)(2,1)} %latents.1) | copy-start | bytes 49156
  6.1 3.9 %collective-permute-start.1 = (bf16[16,1024]{1,0:T(8,128)(2,1)S(1)}, bf16[16,1024]{1,0:T(8,128)(2,1)S(1)}, u32[]{:S(2)}, u32[]{:S(2)}) collective-permute-start(bf16[16,1024]{1,0:T(8,128)(2,1)S(1)} %pad_maximum_fusion.1), channel_id=1, source_target_pairs={{0,4},{2,6},{4,0},{6,2},{8,12},{10,14},{12,8},{14,10},{1,5},{3,7},... | collective-permute-start | bytes 98312 | tf_op jit(solution)/shard_map/ppermute | solution.py:230
  8.0 4.2 %copy-start = (bf16[2,512,1024]{2,1,0:T(8,128)(2,1)S(1)}, bf16[2,512,1024]{2,1,0:T(8,128)(2,1)}, u32[]{:S(2)}) copy-start(bf16[2,512,1024]{2,1,0:T(8,128)(2,1)} %q_own.3) | copy-start | bytes 6291460
  8.0 4.2 %copy-start.1 = (bf16[2,512,1024]{2,1,0:T(8,128)(2,1)S(1)}, bf16[2,512,1024]{2,1,0:T(8,128)(2,1)}, u32[]{:S(2)}) copy-start(bf16[2,512,1024]{2,1,0:T(8,128)(2,1)} %o_own.1) | copy-start | bytes 6291460
  10.0 5.9 %collective-permute-start.5 = (bf16[32,512]{1,0:T(8,128)(2,1)S(1)}, bf16[32,512]{1,0:T(8,128)(2,1)S(1)}, u32[]{:S(2)}, u32[]{:S(2)}) collective-permute-start(bf16[32,512]{1,0:T(8,128)(2,1)S(1)} %get-tuple-element.34), channel_id=1, source_target_pairs={{0,3},{1,2},{2,1},{3,0},{4,7},{5,6},{6,5},{7,4},{8,11},{9,10},{10,... | collective-permute-start | bytes 98312 | tf_op jit(solution)/shard_map/ppermute | solution.py:254
  10.1 3.6 %collective-permute-start.3 = (bf16[32,512]{1,0:T(8,128)(2,1)S(1)}, bf16[32,512]{1,0:T(8,128)(2,1)S(1)}, u32[]{:S(2)}, u32[]{:S(2)}) collective-permute-start(bf16[32,512]{1,0:T(8,128)(2,1)S(1)} %get-tuple-element.34), channel_id=1, source_target_pairs={{0,1},{1,0},{2,3},{3,2},{4,5},{5,4},{6,7},{7,6},{8,9},{9,8},{10,11... | collective-permute-start | bytes 98312 | tf_op jit(solution)/shard_map/ppermute | solution.py:254
  12.0 3.9 %collective-permute-start.4 = (bf16[32,512]{1,0:T(8,128)(2,1)S(1)}, bf16[32,512]{1,0:T(8,128)(2,1)S(1)}, u32[]{:S(2)}, u32[]{:S(2)}) collective-permute-start(bf16[32,512]{1,0:T(8,128)(2,1)S(1)} %get-tuple-element.33), channel_id=1, source_target_pairs={{0,2},{1,3},{2,0},{3,1},{4,6},{5,7},{6,4},{7,5},{8,10},{9,11},{10,... | collective-permute-start | bytes 98312 | tf_op jit(solution)/shard_map/ppermute | solution.py:254
  12.2 3.7 %copy-start.2 = (bf16[2,512,1024]{2,1,0:T(8,128)(2,1)S(1)}, bf16[2,512,1024]{2,1,0:T(8,128)(2,1)}, u32[]{:S(2)}) copy-start(bf16[2,512,1024]{2,1,0:T(8,128)(2,1)} %k_own.1) | copy-start | bytes 6291460
  12.2 3.8 %copy-start.3 = (bf16[2,512,1024]{2,1,0:T(8,128)(2,1)S(1)}, bf16[2,512,1024]{2,1,0:T(8,128)(2,1)}, u32[]{:S(2)}) copy-start(bf16[2,512,1024]{2,1,0:T(8,128)(2,1)} %v_own.1) | copy-start | bytes 6291460
  16.7 2.7 %collective-permute-start.6 = (f32[2,128,1024]{2,1,0:T(8,128)S(1)}, f32[2,128,1024]{2,1,0:T(8,128)S(1)}, u32[]{:S(2)}, u32[]{:S(2)}) collective-permute-start(f32[2,128,1024]{2,1,0:T(8,128)S(1)} %get-tuple-element.41.mine), channel_id=1, source_target_pairs={{0,1},{1,0},{2,3},{3,2},{4,5},{5,4},{6,7},{7,6},{8,9},{9,8},{10,11... | collective-permute-start | bytes 3145736 | tf_op jit(solution)/shard_map/ppermute | solution.py:186
  19.4 2.7 %collective-permute-start.7 = (bf16[512,1024]{1,0:T(8,128)(2,1)S(1)}, bf16[512,1024]{1,0:T(8,128)(2,1)S(1)}, u32[]{:S(2)}, u32[]{:S(2)}) collective-permute-start(bf16[512,1024]{1,0:T(8,128)(2,1)S(1)} %get-tuple-element.44.o_own), channel_id=1, source_target_pairs={{0,1},{1,0},{2,3},{3,2},{4,5},{5,4},{6,7},{7,6},{8,9},{9,8},{10,11... | collective-permute-start | bytes 3145736 | tf_op jit(solution)/shard_map/ppermute | solution.py:186
  22.1 4.0 %collective-permute-start.9 = (bf16[512,1024]{1,0:T(8,128)(2,1)S(1)}, bf16[512,1024]{1,0:T(8,128)(2,1)S(1)}, u32[]{:S(2)}, u32[]{:S(2)}) collective-permute-start(bf16[512,1024]{1,0:T(8,128)(2,1)S(1)} %get-tuple-element.52.o_own), channel_id=1, source_target_pairs={{0,1},{1,0},{2,3},{3,2},{4,5},{5,4},{6,7},{7,6},{8,9},{9,8},{10,11... | collective-permute-start | bytes 3145736 | tf_op jit(solution)/shard_map/ppermute | solution.py:186
  22.2 4.0 %collective-permute-start.8 = (f32[2,128,1024]{2,1,0:T(8,128)S(1)}, f32[2,128,1024]{2,1,0:T(8,128)S(1)}, u32[]{:S(2)}, u32[]{:S(2)}) collective-permute-start(f32[2,128,1024]{2,1,0:T(8,128)S(1)} %get-tuple-element.51.mine), channel_id=1, source_target_pairs={{0,1},{1,0},{2,3},{3,2},{4,5},{5,4},{6,7},{7,6},{8,9},{9,8},{10,11... | collective-permute-start | bytes 3145736 | tf_op jit(solution)/shard_map/ppermute | solution.py:186

commit v4 on v2

--- a/solution.py
+++ b/solution.py
@@ -99,75 +99,98 @@
             target[pair, count : 2 * count, 0:128] = jnp.where(low, zero, piece)
 
 
-def attend(query, ones, key_pairs, value_pairs, attended):
-    pairs, twice, _ = key_pairs.shape
-    count = twice // 2
-    for pair in range(pairs):
-        columns = slice(pair * 128, pair * 128 + 128)
-        scores = dot_t(query[:, columns], key_pairs[pair])
-        expo = []
-        for head in range(2):
-            part = scores[:, head * count : (head + 1) * count]
-            expo.append(jnp.exp(part - jnp.max(part, axis=-1, keepdims=True)).astype(jnp.bfloat16))
-        weights = jnp.concatenate([value_pairs[pair], ones[...]], axis=1)
-        mixed = dot(jnp.concatenate(expo, axis=1), weights)
-        sums = mixed[:, 128:256]
-        inverse = pl.reciprocal(sums, approx=True)
-        inverse = inverse * (2.0 - sums * inverse)
-        attended[:, columns] = (mixed[:, 0:128] * inverse).astype(jnp.bfloat16)
+def attend_pair(query, ones, key_pairs, value_pairs, attended, pair):
+    count = key_pairs.shape[1] // 2
+    columns = slice(pair * 128, pair * 128 + 128)
+    scores = dot_t(query[:, columns], key_pairs[pair])
+    expo = []
+    for head in range(2):
+        part = scores[:, head * count : (head + 1) * count]
+        expo.append(jnp.exp(part - jnp.max(part, axis=-1, keepdims=True)).astype(jnp.bfloat16))
+    weights = jnp.concatenate([value_pairs[pair], ones[...]], axis=1)
+    mixed = dot(jnp.concatenate(expo, axis=1), weights)
+    sums = mixed[:, 128:256]
+    inverse = pl.reciprocal(sums, approx=True)
+    inverse = inverse * (2.0 - sums * inverse)
+    attended[:, columns] = (mixed[:, 0:128] * inverse).astype(jnp.bfloat16)
 
 
 def add_output(state, attended, panel):
     return (state.astype(jnp.float32) + dot(attended, panel)).astype(jnp.bfloat16)
 
 
-def attend_all(query, ones, mine, theirs, key_pairs, value_pairs, attended, block):
-    pair_up(mine, theirs, key_pairs, value_pairs)
-    steps = query.shape[0] // block
-
-    def one_block(step):
-        rows = pl.ds(pl.multiple_of(step * block, block), block)
-        attend(query[rows, :], ones, key_pairs, value_pairs, attended.at[rows, :])
-
-    if steps <= 2:
-        for step in range(steps):
-            one_block(step)
+def attend_and_project(hidden, query, ones, key_pairs, value_pairs, attended, ready, panel, out, block):
+    rows, width = hidden.shape
+    pairs = width // 128
+    chunk = 256
+
+    def attend_rows(place, pair):
+        attend_pair(query.at[place, :], ones, key_pairs, value_pairs, attended.at[place, :], pair)
+
+    def project(place, number):
+        columns = slice(number * chunk, number * chunk + chunk)
+        out[place, columns] = add_output(hidden[place, columns], attended[place, :], panel[:, columns])
+
+    if block == rows:
+        top, bottom = slice(0, rows // 2), slice(rows // 2, rows)
+        for pair in range(pairs):
+            attend_rows(top, pair)
+        ready()
+        for pair in range(pairs):
+            attend_rows(bottom, pair)
+            if pair % 2 == 1:
+                project(top, pair // 2)
+        yield top
+        for number in range(width // chunk):
+            project(bottom, number)
+        yield bottom
     else:
-        pl.loop(0, steps)(one_block)
+
+        @pl.loop(0, rows // block)
+        def _(step):
+            place = pl.ds(pl.multiple_of(step * block, block), block)
+            for pair in range(pairs):
+                attend_rows(place, pair)
+
+        ready()
+        for number in range(width // chunk):
+            project(slice(0, rows), number)
+        yield slice(0, rows)
 
 
 def first_kernel(
     narrow, hidden, query, ones, mine, theirs, gains, q_own, q_other, o_own, o_other, out, next_query,
-    q_panel, o_panel, key_pairs, value_pairs, attended, sems, *, scale, block, dense_block,
+    q_panel, o_panel, key_pairs, value_pairs, attended, sems, *, scale, block,
 ):
     o_copies = fetch(narrow[0], o_own.at[0], o_other.at[0], o_panel, sems.at[0])
     q_copies = fetch(narrow[0], q_own.at[1], q_other.at[1], q_panel, sems.at[1])
-    attend_all(query, ones, mine, theirs, key_pairs, value_pairs, attended, block)
-    finish(o_copies)
-    finish(q_copies)
-
-    @pl.loop(0, hidden.shape[0] // dense_block)
-    def _(step):
-        rows = pl.ds(pl.multiple_of(step * dense_block, dense_block), dense_block)
-        state = add_output(hidden[rows, :], attended[rows, :], o_panel[...])
-        out[rows, :] = state
-        normed = layer_norm(state, gains[1:2, :])
-        next_query[rows, :] = (dot(normed, q_panel[...]) * scale).astype(jnp.bfloat16)
+    pair_up(mine, theirs, key_pairs, value_pairs)
+
+    def ready():
+        finish(o_copies)
+        finish(q_copies)
+
+    normed = []
+    for place in attend_and_project(
+        hidden, query, ones, key_pairs, value_pairs, attended, ready, o_panel, out, block
+    ):
+        normed.append((place, layer_norm(out[place, :], gains[1:2, :])))
+    for place, values in normed:
+        next_query[place, :] = (dot(values, q_panel[...]) * scale).astype(jnp.bfloat16)
 
 
 def last_kernel(
     narrow, hidden, query, ones, mine, theirs, o_own, o_other, out,
-    o_panel, key_pairs, value_pairs, attended, result, sems, out_sems, *, block, chunk,
+    o_panel, key_pairs, value_pairs, attended, result, sems, out_sems, *, block,
 ):
     copies = fetch(narrow[0], o_own.at[1], o_other.at[1], o_panel, sems)
-    attend_all(query, ones, mine, theirs, key_pairs, value_pairs, attended, block)
-    finish(copies)
+    pair_up(mine, theirs, key_pairs, value_pairs)
     leaving = []
-    for step in range(hidden.shape[1] // chunk):
-        columns = slice(step * chunk, step * chunk + chunk)
-        result[:, columns] = add_output(hidden[:, columns], attended[...], o_panel[:, columns])
+    for place in attend_and_project(
+        hidden, query, ones, key_pairs, value_pairs, attended, lambda: finish(copies), o_panel, result, block
+    ):
         leaving.append(
-            pltpu.make_async_copy(result.at[:, columns], out.at[:, columns], out_sems.at[step])
+            pltpu.make_async_copy(result.at[place], out.at[place], out_sems.at[len(leaving)])
         )
         leaving[-1].start()
     finish(leaving)
@@ -186,7 +209,7 @@
         rows, width = queries.shape
         count = latents.shape[0] * wide * 2
         scale = (width // HEADS) ** (-0.5)
-        block = min(256, max(16, 32768 // count))
+        block = rows if count <= 256 else max(16, 32768 // count)
         params = pltpu.CompilerParams(vmem_limit_bytes=GRANT if count <= 256 else LARGE_GRANT)
         panel = pltpu.VMEM((width, width), jnp.bfloat16)
         attended = pltpu.VMEM((rows, width), jnp.bfloat16)
@@ -281,7 +304,7 @@
         second_other = swap(second)
 
         hidden, query = pl.pallas_call(
-            functools.partial(first_kernel, scale=scale, block=block, dense_block=rows),
+            functools.partial(first_kernel, scale=scale, block=block),
             out_shape=(hidden_shape, hidden_shape),
             in_specs=[SMEM] + [VMEM] * 6 + [ANY] * 4,
             out_specs=(VMEM, VMEM),
@@ -290,7 +313,7 @@
             cost_estimate=cost(2 * dense + attend_cost, rows * count * HEADS),
         )(narrow, queries, query, ones, first, first_other, norm_gains, q_weight, q_other, o_weight, o_other)
         return pl.pallas_call(
-            functools.partial(last_kernel, block=block, chunk=256),
+            functools.partial(last_kernel, block=block),
             out_shape=hidden_shape,
             in_specs=[SMEM] + [VMEM] * 5 + [ANY] * 2,
             out_specs=ANY,
@@ -300,7 +323,7 @@
                 attended,
                 pltpu.VMEM((rows, width), jnp.bfloat16),
                 pltpu.SemaphoreType.DMA((2,)),
-                pltpu.SemaphoreType.DMA((width // 256,)),
+                pltpu.SemaphoreType.DMA((2,)),
             ],
             compiler_params=params,
             cost_estimate=cost(attend_cost + dense, rows * count * HEADS),

time: 29.7 us -> 30.4 us (1.024)
  Pallas kernels: 13.2 us -> 14 us
    pallas_call x2, Pallas kernels: 9.79 us -> 10.6 us  [the longest x1 5.58 us: shards(): pl.pallas_call(functools.partial(first_kernel, scale=scale, block=block),...]
  transfers between devices with their start and end apart: 9 -> 9, of which waited for: 4 -> 4; matrix products, arithmetic and copies ran while one was open for 0% -> 0% of each run, Pallas kernels for 29% -> 27%
where the time goes in v4:
time: 30.4 us; the launch traced here: 30.2 us
  Pallas kernels  14 us (46%)
  starting transfers between devices  8.59 us (28%)
  waiting for transfers between devices  6.68 us (22%)
  local copies, waits for them, and re-layouts  0.75 us (2%)
    pallas_call x1, Pallas kernels, shards(): pl.pallas_call(functools.partial(first_kernel, scale=scale, block=block),...  5.58 us
    ppermute x2, starting transfers between devices, shards(): lax.ppermute(source, 'wide', [(i, i ^ step) for i in range(wide)])  5.57 us
    pallas_call x1, Pallas kernels, shards(): pl.pallas_call(functools.partial(last_kernel, block=block), out_shape=hid...  4.99 us
    ppermute x4, waiting for transfers between devices, swap(): return lax.ppermute(array, 'narrow', [(0, 1), (1, 0)])  2.65 us
    ppermute x3, waiting for transfers between devices, shards(): lax.ppermute(array, ('wide', 'narrow'), [(i, i ^ mask) for i in devices])  2.42 us
    ppermute x3, starting transfers between devices, shards(): lax.ppermute(array, ('wide', 'narrow'), [(i, i ^ mask) for i in devices])  2.2 us
    ppermute x2, waiting for transfers between devices, shards(): lax.ppermute(source, 'wide', [(i, i ^ step) for i in range(wide)])  1.61 us
    pallas_call x1, Pallas kernels, shards(): pl.pallas_call(norm_kernel, out_shape=(hidden_shape, jax.ShapeDtypeStruct...  1.38 us
  transfers between devices with their start and end apart: 9, of which 4 were waited for; matrix products, arithmetic and copies ran while one was open for 0% of the time, Pallas kernels for 27%

profile of v4, /device:TPU:0, one launch (start us, length us, event | category | flops | bytes accessed | tf_op | source)
XLA Modules:
  0.0 30.2 jit_solution(8473674800304269548)
XLA Ops:
  0.0 0.5 %collective-permute-start.2 = (bf16[2,512,1024]{2,1,0:T(8,128)(2,1)}, bf16[2,512,1024]{2,1,0:T(8,128)(2,1)}, u32[]{:S(2)}, u32[]{:S(2)}) collective-permute-start(bf16[2,512,1024]{2,1,0:T(8,128)(2,1)} %q_own.3), channel_id=1, source_target_pairs={{0,1},{1,0},{2,3},{3,2},{4,5},{5,4},{6,7},{7,6},{8,9},{9,8},{10,11... | collective-permute-start | bytes 6291464 | tf_op jit(solution)/shard_map/ppermute | solution.py:201
  0.5 3.7 %collective-permute-start = (bf16[8,1024]{1,0:T(8,128)(2,1)}, bf16[8,1024]{1,0:T(8,128)(2,1)S(1)}, u32[]{:S(2)}, u32[]{:S(2)}) collective-permute-start(bf16[8,1024]{1,0:T(8,128)(2,1)} %latents.1), channel_id=1, source_target_pairs={{0,8},{2,10},{4,12},{6,14},{8,0},{10,2},{12,4},{14,6},{1,9},{3,11}... | collective-permute-start | bytes 49160 | tf_op jit(solution)/shard_map/ppermute | solution.py:246
  4.1 0.2 collective-permute-start.6
  4.3 0.7 %copy-done.6 = bf16[8,1024]{1,0:T(8,128)(2,1)S(1)} copy-done((bf16[8,1024]{1,0:T(8,128)(2,1)S(1)}, bf16[8,1024]{1,0:T(8,128)(2,1)}, u32[]{:S(2)}) %copy-start.6) | copy-done | bytes 16408
  5.0 1.0 %collective-permute-done = bf16[8,1024]{1,0:T(8,128)(2,1)S(1)} collective-permute-done((bf16[8,1024]{1,0:T(8,128)(2,1)}, bf16[8,1024]{1,0:T(8,128)(2,1)S(1)}, u32[]{:S(2)}, u32[]{:S(2)}) %collective-permute-start) | collective-permute-done | bytes 16416 | tf_op jit(solution)/shard_map/ppermute | solution.py:246
  6.1 1.9 %collective-permute-start.1 = (bf16[16,1024]{1,0:T(8,128)(2,1)S(1)}, bf16[16,1024]{1,0:T(8,128)(2,1)S(1)}, u32[]{:S(2)}, u32[]{:S(2)}) collective-permute-start(bf16[16,1024]{1,0:T(8,128)(2,1)S(1)} %pad_maximum_fusion.1), channel_id=1, source_target_pairs={{0,4},{2,6},{4,0},{6,2},{8,12},{10,14},{12,8},{14,10},{1,5},{3,7},... | collective-permute-start | bytes 98312 | tf_op jit(solution)/shard_map/ppermute | solution.py:246
  8.0 1.4 %shard_map.74 = (bf16[512,1024]{1,0:T(8,128)(2,1)S(1)}, bf16[512,1024]{1,0:T(8,128)(2,1)S(1)}) custom-call(bf16[512,1024]{1,0:T(8,128)(2,1)S(1)} %copy-done.4, f32[2,1024]{1,0:T(2,128)S(1)} %copy-done.5, bf16[2,512,1024]{2,1,0:T(8,128)(2,1)} %collective-permute-done.2.q_other), custom_call_target="tpu_custom_call" | custom-call | flops 4294967296 | bytes 4194304 | tf_op jit(solution)/shard_map/pallas_call | solution.py:249
  9.4 0.6 %collective-permute-done.1 = bf16[16,1024]{1,0:T(8,128)(2,1)S(1)} collective-permute-done((bf16[16,1024]{1,0:T(8,128)(2,1)S(1)}, bf16[16,1024]{1,0:T(8,128)(2,1)S(1)}, u32[]{:S(2)}, u32[]{:S(2)}) %collective-permute-start.1) | collective-permute-done | bytes 32800 | tf_op jit(solution)/shard_map/ppermute | solution.py:246
  10.0 0.1 collective-permute-start.5
  10.1 1.9 %collective-permute-start.3 = (bf16[32,512]{1,0:T(8,128)(2,1)S(1)}, bf16[32,512]{1,0:T(8,128)(2,1)S(1)}, u32[]{:S(2)}, u32[]{:S(2)}) collective-permute-start(bf16[32,512]{1,0:T(8,128)(2,1)S(1)} %get-tuple-element.28), channel_id=1, source_target_pairs={{0,1},{1,0},{2,3},{3,2},{4,5},{5,4},{6,7},{7,6},{8,9},{9,8},{10,11... | collective-permute-start | bytes 98312 | tf_op jit(solution)/shard_map/ppermute | solution.py:270
  12.0 0.2 collective-permute-start.4
  12.2 1.3 %shard_map.75.query = bf16[512,1024]{1,0:T(8,128)(2,1)S(1)} custom-call(s32[1]{0:T(128)} %bitcast.narrow, bf16[512,1024]{1,0:T(8,128)(2,1)S(1)} %get-tuple-element.29.normed, bf16[2,512,1024]{2,1,0:T(8,128)(2,1)S(1)} %copy-done.1, bf16[512,1024]{1,0:T(8,128)(2,1)S(1)} %get-tuple-element.30.q_other), custom_call_target="tpu_custom_call" | custom-call | flops 1073741824 | bytes 4194304 | tf_op jit(solution)/shard_map/pallas_call | solution.py:283
  13.5 0.0 collective-permute-done.3
  13.5 2.4 %collective-permute-done.4 = bf16[32,512]{1,0:T(8,128)(2,1)S(1)} collective-permute-done((bf16[32,512]{1,0:T(8,128)(2,1)S(1)}, bf16[32,512]{1,0:T(8,128)(2,1)S(1)}, u32[]{:S(2)}, u32[]{:S(2)}) %collective-permute-start.4) | collective-permute-done | bytes 32800 | tf_op jit(solution)/shard_map/ppermute | solution.py:270
  15.9 0.0 collective-permute-done.5
  15.9 0.0 copy-start
  15.9 0.0 collective-permute-done.6.o_other
  16.0 0.8 %shard_map.76 = (f32[2,128,1024]{2,1,0:T(8,128)S(1)}, f32[2,128,1024]{2,1,0:T(8,128)S(1)}) custom-call(bf16[128,512]{1,0:T(8,128)(2,1)S(1)} %pad_maximum_fusion.latents, bf16[2,512,1024]{2,1,0:T(8,128)(2,1)S(1)} %copy-done.2, bf16[2,512,1024]{2,1,0:T(8,128)(2,1)S(1)} %copy-done.3), custom_call_target="tpu_custom_call" | custom-call | flops 536870912 | bytes 4194304 | tf_op jit(solution)/shard_map/pallas_call | solution.py:294
  16.7 0.1 collective-permute-start.7
  16.8 2.6 %collective-permute-done.7.theirs = f32[2,128,1024]{2,1,0:T(8,128)S(1)} collective-permute-done((f32[2,128,1024]{2,1,0:T(8,128)S(1)}, f32[2,128,1024]{2,1,0:T(8,128)S(1)}, u32[]{:S(2)}, u32[]{:S(2)}) %collective-permute-start.7) | collective-permute-done | bytes 1048608 | tf_op jit(solution)/shard_map/ppermute | solution.py:201
  19.5 0.1 collective-permute-start.8
  19.6 5.6 %shard_map.77 = (bf16[512,1024]{1,0:T(8,128)(2,1)S(1)}, bf16[512,1024]{1,0:T(8,128)(2,1)S(1)}) custom-call(s32[1]{0:T(128)} %bitcast.narrow, bf16[512,1024]{1,0:T(8,128)(2,1)S(1)} %copy-done.4, bf16[512,1024]{1,0:T(8,128)(2,1)S(1)} %shard_map.75.query, bf16[256,128]{1,0:T(8,128)(2,1)S(1)} %get-tuple-element.32.ones, ...), custom_call_target="tpu_custom_call" | custom-call | flops 2684354560 | bytes 4194304 | tf_op jit(solution)/shard_map/pallas_call | solution.py:306
  25.2 0.0 collective-permute-done.8.theirs
  25.2 5.0 %shard_map.78 = bf16[512,1024]{1,0:T(8,128)(2,1)} custom-call(s32[1]{0:T(128)} %bitcast.narrow, bf16[512,1024]{1,0:T(8,128)(2,1)S(1)} %get-tuple-element.38.hidden, bf16[512,1024]{1,0:T(8,128)(2,1)S(1)} %get-tuple-element.39.query, bf16[256,128]{1,0:T(8,128)(2,1)S(1)} %get-tuple-element.32.ones, f32[2,128,1024]{2,1,0:T(8,128)S(1)} %get-tuple-element.40.mine, ...), custom_call_target="tpu_custom_call" | custom-call | flops 1610612736 | bytes 4194304 | tf_op jit(solution)/shard_map/pallas_call | solution.py:315
  (22 shorter events, 0.1 us)
Async XLA Ops:
  0.0 8.0 %copy-start.5 = (f32[2,1024]{1,0:T(2,128)S(1)}, f32[2,1024]{1,0:T(2,128)}, u32[]{:S(2)}) copy-start(f32[2,1024]{1,0:T(2,128)} %gains.3) | copy-start | bytes 24580
  0.0 8.0 %copy-start.4 = (bf16[512,1024]{1,0:T(8,128)(2,1)S(1)}, bf16[512,1024]{1,0:T(8,128)(2,1)}, u32[]{:S(2)}) copy-start(bf16[512,1024]{1,0:T(8,128)(2,1)} %hidden.3) | copy-start | bytes 3145732
  0.0 8.0 %collective-permute-start.2 = (bf16[2,512,1024]{2,1,0:T(8,128)(2,1)}, bf16[2,512,1024]{2,1,0:T(8,128)(2,1)}, u32[]{:S(2)}, u32[]{:S(2)}) collective-permute-start(bf16[2,512,1024]{2,1,0:T(8,128)(2,1)} %q_own.3), channel_id=1, source_target_pairs={{0,1},{1,0},{2,3},{3,2},{4,5},{5,4},{6,7},{7,6},{8,9},{9,8},{10,11... | collective-permute-start | bytes 6291464 | tf_op jit(solution)/shard_map/ppermute | solution.py:201
  0.5 5.6 %collective-permute-start = (bf16[8,1024]{1,0:T(8,128)(2,1)}, bf16[8,1024]{1,0:T(8,128)(2,1)S(1)}, u32[]{:S(2)}, u32[]{:S(2)}) collective-permute-start(bf16[8,1024]{1,0:T(8,128)(2,1)} %latents.1), channel_id=1, source_target_pairs={{0,8},{2,10},{4,12},{6,14},{8,0},{10,2},{12,4},{14,6},{1,9},{3,11}... | collective-permute-start | bytes 49160 | tf_op jit(solution)/shard_map/ppermute | solution.py:246
  4.1 11.8 %collective-permute-start.6 = (bf16[2,512,1024]{2,1,0:T(8,128)(2,1)}, bf16[2,512,1024]{2,1,0:T(8,128)(2,1)S(1)}, u32[]{:S(2)}, u32[]{:S(2)}) collective-permute-start(bf16[2,512,1024]{2,1,0:T(8,128)(2,1)} %o_own.3), channel_id=1, source_target_pairs={{0,1},{1,0},{2,3},{3,2},{4,5},{5,4},{6,7},{7,6},{8,9},{9,8},{10,11... | collective-permute-start | bytes 6291464 | tf_op jit(solution)/shard_map/ppermute | solution.py:201
  4.3 0.7 %copy-start.6 = (bf16[8,1024]{1,0:T(8,128)(2,1)S(1)}, bf16[8,1024]{1,0:T(8,128)(2,1)}, u32[]{:S(2)}) copy-start(bf16[8,1024]{1,0:T(8,128)(2,1)} %latents.1) | copy-start | bytes 49156
  6.1 3.9 %collective-permute-start.1 = (bf16[16,1024]{1,0:T(8,128)(2,1)S(1)}, bf16[16,1024]{1,0:T(8,128)(2,1)S(1)}, u32[]{:S(2)}, u32[]{:S(2)}) collective-permute-start(bf16[16,1024]{1,0:T(8,128)(2,1)S(1)} %pad_maximum_fusion.1), channel_id=1, source_target_pairs={{0,4},{2,6},{4,0},{6,2},{8,12},{10,14},{12,8},{14,10},{1,5},{3,7},... | collective-permute-start | bytes 98312 | tf_op jit(solution)/shard_map/ppermute | solution.py:246
  8.0 4.2 %copy-start.1 = (bf16[2,512,1024]{2,1,0:T(8,128)(2,1)S(1)}, bf16[2,512,1024]{2,1,0:T(8,128)(2,1)}, u32[]{:S(2)}) copy-start(bf16[2,512,1024]{2,1,0:T(8,128)(2,1)} %q_own.3) | copy-start | bytes 6291460
  10.0 5.9 %collective-permute-start.5 = (bf16[32,512]{1,0:T(8,128)(2,1)S(1)}, bf16[32,512]{1,0:T(8,128)(2,1)S(1)}, u32[]{:S(2)}, u32[]{:S(2)}) collective-permute-start(bf16[32,512]{1,0:T(8,128)(2,1)S(1)} %get-tuple-element.28), channel_id=1, source_target_pairs={{0,3},{1,2},{2,1},{3,0},{4,7},{5,6},{6,5},{7,4},{8,11},{9,10},{10,... | collective-permute-start | bytes 98312 | tf_op jit(solution)/shard_map/ppermute | solution.py:270
  10.1 3.4 %collective-permute-start.3 = (bf16[32,512]{1,0:T(8,128)(2,1)S(1)}, bf16[32,512]{1,0:T(8,128)(2,1)S(1)}, u32[]{:S(2)}, u32[]{:S(2)}) collective-permute-start(bf16[32,512]{1,0:T(8,128)(2,1)S(1)} %get-tuple-element.28), channel_id=1, source_target_pairs={{0,1},{1,0},{2,3},{3,2},{4,5},{5,4},{6,7},{7,6},{8,9},{9,8},{10,11... | collective-permute-start | bytes 98312 | tf_op jit(solution)/shard_map/ppermute | solution.py:270
  12.0 3.9 %collective-permute-start.4 = (bf16[32,512]{1,0:T(8,128)(2,1)S(1)}, bf16[32,512]{1,0:T(8,128)(2,1)S(1)}, u32[]{:S(2)}, u32[]{:S(2)}) collective-permute-start(bf16[32,512]{1,0:T(8,128)(2,1)S(1)} %get-tuple-element.27), channel_id=1, source_target_pairs={{0,2},{1,3},{2,0},{3,1},{4,6},{5,7},{6,4},{7,5},{8,10},{9,11},{10,... | collective-permute-start | bytes 98312 | tf_op jit(solution)/shard_map/ppermute | solution.py:270
  12.2 3.8 %copy-start.2 = (bf16[2,512,1024]{2,1,0:T(8,128)(2,1)S(1)}, bf16[2,512,1024]{2,1,0:T(8,128)(2,1)}, u32[]{:S(2)}) copy-start(bf16[2,512,1024]{2,1,0:T(8,128)(2,1)} %k_own.1) | copy-start | bytes 6291460
  12.2 3.8 %copy-start.3 = (bf16[2,512,1024]{2,1,0:T(8,128)(2,1)S(1)}, bf16[2,512,1024]{2,1,0:T(8,128)(2,1)}, u32[]{:S(2)}) copy-start(bf16[2,512,1024]{2,1,0:T(8,128)(2,1)} %v_own.1) | copy-start | bytes 6291460
  15.9 3.7 %copy-start = (bf16[2,512,1024]{2,1,0:T(8,128)(2,1)S(1)}, bf16[2,512,1024]{2,1,0:T(8,128)(2,1)}, u32[]{:S(2)}) copy-start(bf16[2,512,1024]{2,1,0:T(8,128)(2,1)} %o_own.3) | copy-start | bytes 6291460
  16.7 2.7 %collective-permute-start.7 = (f32[2,128,1024]{2,1,0:T(8,128)S(1)}, f32[2,128,1024]{2,1,0:T(8,128)S(1)}, u32[]{:S(2)}, u32[]{:S(2)}) collective-permute-start(f32[2,128,1024]{2,1,0:T(8,128)S(1)} %get-tuple-element.34.mine), channel_id=1, source_target_pairs={{0,1},{1,0},{2,3},{3,2},{4,5},{5,4},{6,7},{7,6},{8,9},{9,8},{10,11... | collective-permute-start | bytes 3145736 | tf_op jit(solution)/shard_map/ppermute | solution.py:201
  19.5 5.7 %collective-permute-start.8 = (f32[2,128,1024]{2,1,0:T(8,128)S(1)}, f32[2,128,1024]{2,1,0:T(8,128)S(1)}, u32[]{:S(2)}, u32[]{:S(2)}) collective-permute-start(f32[2,128,1024]{2,1,0:T(8,128)S(1)} %get-tuple-element.40.mine), channel_id=1, source_target_pairs={{0,1},{1,0},{2,3},{3,2},{4,5},{5,4},{6,7},{7,6},{8,9},{9,8},{10,11... | collective-permute-start | bytes 3145736 | tf_op jit(solution)/shard_map/ppermute | solution.py:201

commit v5 on v2

--- a/solution.py
+++ b/solution.py
@@ -138,21 +138,17 @@
 
 def first_kernel(
     narrow, hidden, query, ones, mine, theirs, gains, q_own, q_other, o_own, o_other, out, next_query,
-    q_panel, o_panel, key_pairs, value_pairs, attended, sems, *, scale, block, dense_block,
+    q_panel, o_panel, key_pairs, value_pairs, attended, sems, *, scale, block,
 ):
     o_copies = fetch(narrow[0], o_own.at[0], o_other.at[0], o_panel, sems.at[0])
     q_copies = fetch(narrow[0], q_own.at[1], q_other.at[1], q_panel, sems.at[1])
     attend_all(query, ones, mine, theirs, key_pairs, value_pairs, attended, block)
     finish(o_copies)
+    state = add_output(hidden[...], attended[...], o_panel[...])
+    out[...] = state
+    normed = layer_norm(state, gains[1:2, :])
     finish(q_copies)
-
-    @pl.loop(0, hidden.shape[0] // dense_block)
-    def _(step):
-        rows = pl.ds(pl.multiple_of(step * dense_block, dense_block), dense_block)
-        state = add_output(hidden[rows, :], attended[rows, :], o_panel[...])
-        out[rows, :] = state
-        normed = layer_norm(state, gains[1:2, :])
-        next_query[rows, :] = (dot(normed, q_panel[...]) * scale).astype(jnp.bfloat16)
+    next_query[...] = (dot(normed, q_panel[...]) * scale).astype(jnp.bfloat16)
 
 
 def last_kernel(
@@ -186,7 +182,7 @@
         rows, width = queries.shape
         count = latents.shape[0] * wide * 2
         scale = (width // HEADS) ** (-0.5)
-        block = min(256, max(16, 32768 // count))
+        block = rows if count <= 256 else max(16, 32768 // count)
         params = pltpu.CompilerParams(vmem_limit_bytes=GRANT if count <= 256 else LARGE_GRANT)
         panel = pltpu.VMEM((width, width), jnp.bfloat16)
         attended = pltpu.VMEM((rows, width), jnp.bfloat16)
@@ -249,10 +245,10 @@
         )
         gathered = jnp.concatenate(
             [
+                jnp.where(core == 0, along, across),
+                jnp.where(core == 0, across, along),
                 jnp.where(core == 0, keep, beside),
                 jnp.where(core == 0, beside, keep),
-                jnp.where(core == 0, along, across),
-                jnp.where(core == 0, across, along),
             ],
             axis=0,
         )
@@ -281,7 +277,7 @@
         second_other = swap(second)
 
         hidden, query = pl.pallas_call(
-            functools.partial(first_kernel, scale=scale, block=block, dense_block=rows),
+            functools.partial(first_kernel, scale=scale, block=block),
             out_shape=(hidden_shape, hidden_shape),
             in_specs=[SMEM] + [VMEM] * 6 + [ANY] * 4,
             out_specs=(VMEM, VMEM),

time: 29.7 us -> 29 us (0.976)
  Pallas kernels: 13.2 us -> 12.5 us
    pallas_call x1, Pallas kernels: 5.79 us -> 5.08 us  [shards(): pl.pallas_call(functools.partial(first_kernel, scale=scale, block=block),...]
  transfers between devices with their start and end apart: 9 -> 9, of which waited for: 4 -> 4; matrix products, arithmetic and copies ran while one was open for 0% -> 0% of each run, Pallas kernels for 29% -> 27%
where the time goes in v5:
time: 29 us; the launch traced here: 28.8 us
  Pallas kernels  12.5 us (43%)
  starting transfers between devices  8.61 us (30%)
  waiting for transfers between devices  6.67 us (23%)
  local copies, waits for them, and re-layouts  0.75 us (3%)
    ppermute x2, starting transfers between devices, shards(): lax.ppermute(source, 'wide', [(i, i ^ step) for i in range(wide)])  5.57 us
    pallas_call x1, Pallas kernels, shards(): pl.pallas_call(functools.partial(first_kernel, scale=scale, block=block),...  5.08 us
    pallas_call x1, Pallas kernels, shards(): pl.pallas_call(functools.partial(last_kernel, block=block, chunk=256), ou...  4.04 us
    ppermute x4, waiting for transfers between devices, swap(): return lax.ppermute(array, 'narrow', [(0, 1), (1, 0)])  2.65 us
    ppermute x3, waiting for transfers between devices, shards(): lax.ppermute(array, ('wide', 'narrow'), [(i, i ^ mask) for i in devices])  2.41 us
    ppermute x3, starting transfers between devices, shards(): lax.ppermute(array, ('wide', 'narrow'), [(i, i ^ mask) for i in devices])  2.21 us
    ppermute x2, waiting for transfers between devices, shards(): lax.ppermute(source, 'wide', [(i, i ^ step) for i in range(wide)])  1.61 us
    pallas_call x1, Pallas kernels, shards(): pl.pallas_call(norm_kernel, out_shape=(hidden_shape, jax.ShapeDtypeStruct...  1.38 us
  transfers between devices with their start and end apart: 9, of which 4 were waited for; matrix products, arithmetic and copies ran while one was open for 0% of the time, Pallas kernels for 27%

profile of v5, /device:TPU:0, one launch (start us, length us, event | category | flops | bytes accessed | tf_op | source)
XLA Modules:
  0.0 28.8 jit_solution(15726385327215693944)
XLA Ops:
  0.0 0.5 %collective-permute-start.2 = (bf16[2,512,1024]{2,1,0:T(8,128)(2,1)}, bf16[2,512,1024]{2,1,0:T(8,128)(2,1)}, u32[]{:S(2)}, u32[]{:S(2)}) collective-permute-start(bf16[2,512,1024]{2,1,0:T(8,128)(2,1)} %q_own.3), channel_id=1, source_target_pairs={{0,1},{1,0},{2,3},{3,2},{4,5},{5,4},{6,7},{7,6},{8,9},{9,8},{10,11... | collective-permute-start | bytes 6291464 | tf_op jit(solution)/shard_map/ppermute | solution.py:174
  0.5 3.7 %collective-permute-start = (bf16[8,1024]{1,0:T(8,128)(2,1)}, bf16[8,1024]{1,0:T(8,128)(2,1)S(1)}, u32[]{:S(2)}, u32[]{:S(2)}) collective-permute-start(bf16[8,1024]{1,0:T(8,128)(2,1)} %latents.1), channel_id=1, source_target_pairs={{0,8},{2,10},{4,12},{6,14},{8,0},{10,2},{12,4},{14,6},{1,9},{3,11}... | collective-permute-start | bytes 49160 | tf_op jit(solution)/shard_map/ppermute | solution.py:219
  4.1 0.2 collective-permute-start.6
  4.3 0.7 %copy-done.6 = bf16[8,1024]{1,0:T(8,128)(2,1)S(1)} copy-done((bf16[8,1024]{1,0:T(8,128)(2,1)S(1)}, bf16[8,1024]{1,0:T(8,128)(2,1)}, u32[]{:S(2)}) %copy-start.6) | copy-done | bytes 16408
  5.0 1.0 %collective-permute-done = bf16[8,1024]{1,0:T(8,128)(2,1)S(1)} collective-permute-done((bf16[8,1024]{1,0:T(8,128)(2,1)}, bf16[8,1024]{1,0:T(8,128)(2,1)S(1)}, u32[]{:S(2)}, u32[]{:S(2)}) %collective-permute-start) | collective-permute-done | bytes 16416 | tf_op jit(solution)/shard_map/ppermute | solution.py:219
  6.1 1.9 %collective-permute-start.1 = (bf16[16,1024]{1,0:T(8,128)(2,1)S(1)}, bf16[16,1024]{1,0:T(8,128)(2,1)S(1)}, u32[]{:S(2)}, u32[]{:S(2)}) collective-permute-start(bf16[16,1024]{1,0:T(8,128)(2,1)S(1)} %pad_maximum_fusion.1), channel_id=1, source_target_pairs={{0,4},{2,6},{4,0},{6,2},{8,12},{10,14},{12,8},{14,10},{1,5},{3,7},... | collective-permute-start | bytes 98312 | tf_op jit(solution)/shard_map/ppermute | solution.py:219
  8.0 0.0 collective-permute-done.2.q_other
  8.0 1.4 %shard_map.74 = (bf16[512,1024]{1,0:T(8,128)(2,1)S(1)}, bf16[512,1024]{1,0:T(8,128)(2,1)S(1)}) custom-call(bf16[512,1024]{1,0:T(8,128)(2,1)S(1)} %copy-done.4, f32[2,1024]{1,0:T(2,128)S(1)} %copy-done.5, bf16[2,512,1024]{2,1,0:T(8,128)(2,1)} %collective-permute-done.2.q_other), custom_call_target="tpu_custom_call" | custom-call | flops 4294967296 | bytes 4194304 | tf_op jit(solution)/shard_map/pallas_call | solution.py:222
  9.4 0.6 %collective-permute-done.1 = bf16[16,1024]{1,0:T(8,128)(2,1)S(1)} collective-permute-done((bf16[16,1024]{1,0:T(8,128)(2,1)S(1)}, bf16[16,1024]{1,0:T(8,128)(2,1)S(1)}, u32[]{:S(2)}, u32[]{:S(2)}) %collective-permute-start.1) | collective-permute-done | bytes 32800 | tf_op jit(solution)/shard_map/ppermute | solution.py:219
  10.0 0.1 collective-permute-start.5
  10.1 1.9 %collective-permute-start.4 = (bf16[32,512]{1,0:T(8,128)(2,1)S(1)}, bf16[32,512]{1,0:T(8,128)(2,1)S(1)}, u32[]{:S(2)}, u32[]{:S(2)}) collective-permute-start(bf16[32,512]{1,0:T(8,128)(2,1)S(1)} %get-tuple-element.28), channel_id=1, source_target_pairs={{0,3},{1,2},{2,1},{3,0},{4,7},{5,6},{6,5},{7,4},{8,11},{9,10},{10,... | collective-permute-start | bytes 98312 | tf_op jit(solution)/shard_map/ppermute | solution.py:243
  12.0 0.2 collective-permute-start.3
  12.2 1.3 %shard_map.75.query = bf16[512,1024]{1,0:T(8,128)(2,1)S(1)} custom-call(s32[1]{0:T(128)} %bitcast.narrow, bf16[512,1024]{1,0:T(8,128)(2,1)S(1)} %get-tuple-element.29.normed, bf16[2,512,1024]{2,1,0:T(8,128)(2,1)S(1)} %copy-done.1, bf16[512,1024]{1,0:T(8,128)(2,1)S(1)} %get-tuple-element.30.q_other), custom_call_target="tpu_custom_call" | custom-call | flops 1073741824 | bytes 4194304 | tf_op jit(solution)/shard_map/pallas_call | solution.py:256
  13.5 0.0 collective-permute-done.5
  13.5 2.4 %collective-permute-done.3 = bf16[32,512]{1,0:T(8,128)(2,1)S(1)} collective-permute-done((bf16[32,512]{1,0:T(8,128)(2,1)S(1)}, bf16[32,512]{1,0:T(8,128)(2,1)S(1)}, u32[]{:S(2)}, u32[]{:S(2)}) %collective-permute-start.3) | collective-permute-done | bytes 32800 | tf_op jit(solution)/shard_map/ppermute | solution.py:243
  15.9 0.0 collective-permute-done.4
  16.0 0.0 copy-start
  16.0 0.0 collective-permute-done.6.o_other
  16.0 0.8 %shard_map.76 = (f32[2,128,1024]{2,1,0:T(8,128)S(1)}, f32[2,128,1024]{2,1,0:T(8,128)S(1)}) custom-call(bf16[128,512]{1,0:T(8,128)(2,1)S(1)} %pad_maximum_fusion.latents, bf16[2,512,1024]{2,1,0:T(8,128)(2,1)S(1)} %copy-done.2, bf16[2,512,1024]{2,1,0:T(8,128)(2,1)S(1)} %copy-done.3), custom_call_target="tpu_custom_call" | custom-call | flops 536870912 | bytes 4194304 | tf_op jit(solution)/shard_map/pallas_call | solution.py:267
  16.8 0.1 collective-permute-start.7
  16.8 2.6 %collective-permute-done.7.theirs = f32[2,128,1024]{2,1,0:T(8,128)S(1)} collective-permute-done((f32[2,128,1024]{2,1,0:T(8,128)S(1)}, f32[2,128,1024]{2,1,0:T(8,128)S(1)}, u32[]{:S(2)}, u32[]{:S(2)}) %collective-permute-start.7) | collective-permute-done | bytes 1048608 | tf_op jit(solution)/shard_map/ppermute | solution.py:174
  19.5 0.1 collective-permute-start.8
  19.6 5.1 %shard_map.77 = (bf16[512,1024]{1,0:T(8,128)(2,1)S(1)}, bf16[512,1024]{1,0:T(8,128)(2,1)S(1)}) custom-call(s32[1]{0:T(128)} %bitcast.narrow, bf16[512,1024]{1,0:T(8,128)(2,1)S(1)} %copy-done.4, bf16[512,1024]{1,0:T(8,128)(2,1)S(1)} %shard_map.75.query, bf16[256,128]{1,0:T(8,128)(2,1)S(1)} %get-tuple-element.32.ones, ...), custom_call_target="tpu_custom_call" | custom-call | flops 2684354560 | bytes 4194304 | tf_op jit(solution)/shard_map/pallas_call | solution.py:279
  24.7 4.0 %shard_map.78 = bf16[512,1024]{1,0:T(8,128)(2,1)} custom-call(s32[1]{0:T(128)} %bitcast.narrow, bf16[512,1024]{1,0:T(8,128)(2,1)S(1)} %get-tuple-element.38.hidden, bf16[512,1024]{1,0:T(8,128)(2,1)S(1)} %get-tuple-element.39.query, bf16[256,128]{1,0:T(8,128)(2,1)S(1)} %get-tuple-element.32.ones, f32[2,128,1024]{2,1,0:T(8,128)S(1)} %get-tuple-element.40.mine, ...), custom_call_target="tpu_custom_call" | custom-call | flops 1610612736 | bytes 4194304 | tf_op jit(solution)/shard_map/pallas_call | solution.py:288
  (22 shorter events, 0.1 us)
Async XLA Ops:
  0.0 8.0 %copy-start.5 = (f32[2,1024]{1,0:T(2,128)S(1)}, f32[2,1024]{1,0:T(2,128)}, u32[]{:S(2)}) copy-start(f32[2,1024]{1,0:T(2,128)} %gains.3) | copy-start | bytes 24580
  0.0 8.0 %copy-start.4 = (bf16[512,1024]{1,0:T(8,128)(2,1)S(1)}, bf16[512,1024]{1,0:T(8,128)(2,1)}, u32[]{:S(2)}) copy-start(bf16[512,1024]{1,0:T(8,128)(2,1)} %hidden.3) | copy-start | bytes 3145732
  0.0 8.0 %collective-permute-start.2 = (bf16[2,512,1024]{2,1,0:T(8,128)(2,1)}, bf16[2,512,1024]{2,1,0:T(8,128)(2,1)}, u32[]{:S(2)}, u32[]{:S(2)}) collective-permute-start(bf16[2,512,1024]{2,1,0:T(8,128)(2,1)} %q_own.3), channel_id=1, source_target_pairs={{0,1},{1,0},{2,3},{3,2},{4,5},{5,4},{6,7},{7,6},{8,9},{9,8},{10,11... | collective-permute-start | bytes 6291464 | tf_op jit(solution)/shard_map/ppermute | solution.py:174
  0.5 5.6 %collective-permute-start = (bf16[8,1024]{1,0:T(8,128)(2,1)}, bf16[8,1024]{1,0:T(8,128)(2,1)S(1)}, u32[]{:S(2)}, u32[]{:S(2)}) collective-permute-start(bf16[8,1024]{1,0:T(8,128)(2,1)} %latents.1), channel_id=1, source_target_pairs={{0,8},{2,10},{4,12},{6,14},{8,0},{10,2},{12,4},{14,6},{1,9},{3,11}... | collective-permute-start | bytes 49160 | tf_op jit(solution)/shard_map/ppermute | solution.py:219
  4.1 11.8 %collective-permute-start.6 = (bf16[2,512,1024]{2,1,0:T(8,128)(2,1)}, bf16[2,512,1024]{2,1,0:T(8,128)(2,1)S(1)}, u32[]{:S(2)}, u32[]{:S(2)}) collective-permute-start(bf16[2,512,1024]{2,1,0:T(8,128)(2,1)} %o_own.3), channel_id=1, source_target_pairs={{0,1},{1,0},{2,3},{3,2},{4,5},{5,4},{6,7},{7,6},{8,9},{9,8},{10,11... | collective-permute-start | bytes 6291464 | tf_op jit(solution)/shard_map/ppermute | solution.py:174
  4.3 0.7 %copy-start.6 = (bf16[8,1024]{1,0:T(8,128)(2,1)S(1)}, bf16[8,1024]{1,0:T(8,128)(2,1)}, u32[]{:S(2)}) copy-start(bf16[8,1024]{1,0:T(8,128)(2,1)} %latents.1) | copy-start | bytes 49156
  6.1 3.9 %collective-permute-start.1 = (bf16[16,1024]{1,0:T(8,128)(2,1)S(1)}, bf16[16,1024]{1,0:T(8,128)(2,1)S(1)}, u32[]{:S(2)}, u32[]{:S(2)}) collective-permute-start(bf16[16,1024]{1,0:T(8,128)(2,1)S(1)} %pad_maximum_fusion.1), channel_id=1, source_target_pairs={{0,4},{2,6},{4,0},{6,2},{8,12},{10,14},{12,8},{14,10},{1,5},{3,7},... | collective-permute-start | bytes 98312 | tf_op jit(solution)/shard_map/ppermute | solution.py:219
  8.0 4.2 %copy-start.1 = (bf16[2,512,1024]{2,1,0:T(8,128)(2,1)S(1)}, bf16[2,512,1024]{2,1,0:T(8,128)(2,1)}, u32[]{:S(2)}) copy-start(bf16[2,512,1024]{2,1,0:T(8,128)(2,1)} %q_own.3) | copy-start | bytes 6291460
  10.0 3.5 %collective-permute-start.5 = (bf16[32,512]{1,0:T(8,128)(2,1)S(1)}, bf16[32,512]{1,0:T(8,128)(2,1)S(1)}, u32[]{:S(2)}, u32[]{:S(2)}) collective-permute-start(bf16[32,512]{1,0:T(8,128)(2,1)S(1)} %get-tuple-element.28), channel_id=1, source_target_pairs={{0,1},{1,0},{2,3},{3,2},{4,5},{5,4},{6,7},{7,6},{8,9},{9,8},{10,11... | collective-permute-start | bytes 98312 | tf_op jit(solution)/shard_map/ppermute | solution.py:243
  10.1 5.9 %collective-permute-start.4 = (bf16[32,512]{1,0:T(8,128)(2,1)S(1)}, bf16[32,512]{1,0:T(8,128)(2,1)S(1)}, u32[]{:S(2)}, u32[]{:S(2)}) collective-permute-start(bf16[32,512]{1,0:T(8,128)(2,1)S(1)} %get-tuple-element.28), channel_id=1, source_target_pairs={{0,3},{1,2},{2,1},{3,0},{4,7},{5,6},{6,5},{7,4},{8,11},{9,10},{10,... | collective-permute-start | bytes 98312 | tf_op jit(solution)/shard_map/ppermute | solution.py:243
  12.0 3.9 %collective-permute-start.3 = (bf16[32,512]{1,0:T(8,128)(2,1)S(1)}, bf16[32,512]{1,0:T(8,128)(2,1)S(1)}, u32[]{:S(2)}, u32[]{:S(2)}) collective-permute-start(bf16[32,512]{1,0:T(8,128)(2,1)S(1)} %get-tuple-element.27), channel_id=1, source_target_pairs={{0,2},{1,3},{2,0},{3,1},{4,6},{5,7},{6,4},{7,5},{8,10},{9,11},{10,... | collective-permute-start | bytes 98312 | tf_op jit(solution)/shard_map/ppermute | solution.py:243
  12.2 3.8 %copy-start.2 = (bf16[2,512,1024]{2,1,0:T(8,128)(2,1)S(1)}, bf16[2,512,1024]{2,1,0:T(8,128)(2,1)}, u32[]{:S(2)}) copy-start(bf16[2,512,1024]{2,1,0:T(8,128)(2,1)} %k_own.1) | copy-start | bytes 6291460
  12.2 3.8 %copy-start.3 = (bf16[2,512,1024]{2,1,0:T(8,128)(2,1)S(1)}, bf16[2,512,1024]{2,1,0:T(8,128)(2,1)}, u32[]{:S(2)}) copy-start(bf16[2,512,1024]{2,1,0:T(8,128)(2,1)} %v_own.1) | copy-start | bytes 6291460
  16.0 3.7 %copy-start = (bf16[2,512,1024]{2,1,0:T(8,128)(2,1)S(1)}, bf16[2,512,1024]{2,1,0:T(8,128)(2,1)}, u32[]{:S(2)}) copy-start(bf16[2,512,1024]{2,1,0:T(8,128)(2,1)} %o_own.3) | copy-start | bytes 6291460
  16.8 2.7 %collective-permute-start.7 = (f32[2,128,1024]{2,1,0:T(8,128)S(1)}, f32[2,128,1024]{2,1,0:T(8,128)S(1)}, u32[]{:S(2)}, u32[]{:S(2)}) collective-permute-start(f32[2,128,1024]{2,1,0:T(8,128)S(1)} %get-tuple-element.34.mine), channel_id=1, source_target_pairs={{0,1},{1,0},{2,3},{3,2},{4,5},{5,4},{6,7},{7,6},{8,9},{9,8},{10,11... | collective-permute-start | bytes 3145736 | tf_op jit(solution)/shard_map/ppermute | solution.py:174
  19.5 5.2 %collective-permute-start.8 = (f32[2,128,1024]{2,1,0:T(8,128)S(1)}, f32[2,128,1024]{2,1,0:T(8,128)S(1)}, u32[]{:S(2)}, u32[]{:S(2)}) collective-permute-start(f32[2,128,1024]{2,1,0:T(8,128)S(1)} %get-tuple-element.40.mine), channel_id=1, source_target_pairs={{0,1},{1,0},{2,3},{3,2},{4,5},{5,4},{6,7},{7,6},{8,9},{9,8},{10,11... | collective-permute-start | bytes 3145736 | tf_op jit(solution)/shard_map/ppermute | solution.py:174

commit v6 on v5

--- a/solution.py
+++ b/solution.py
@@ -81,10 +81,9 @@
         out[rows, :] = (query * scale).astype(jnp.bfloat16)
 
 
-def latent_kernel(latents, k_own, v_own, first, second):
-    for layer, target in enumerate((first, second)):
-        for i, own in enumerate((k_own, v_own)):
-            target[i] = dot(latents[...], own[layer])
+def latent_kernel(latents, k_own, v_own, out, *, layer):
+    for i, own in enumerate((k_own, v_own)):
+        out[i] = dot(latents[...], own[layer])
 
 
 def pair_up(mine, theirs, key_pairs, value_pairs):
@@ -144,11 +143,13 @@
     q_copies = fetch(narrow[0], q_own.at[1], q_other.at[1], q_panel, sems.at[1])
     attend_all(query, ones, mine, theirs, key_pairs, value_pairs, attended, block)
     finish(o_copies)
-    state = add_output(hidden[...], attended[...], o_panel[...])
-    out[...] = state
-    normed = layer_norm(state, gains[1:2, :])
+    chunks = [slice(i, i + 256) for i in range(0, hidden.shape[1], 256)]
+    for columns in chunks:
+        out[:, columns] = add_output(hidden[:, columns], attended[...], o_panel[:, columns])
+    normed = layer_norm(out[...], gains[1:2, :])
     finish(q_copies)
-    next_query[...] = (dot(normed, q_panel[...]) * scale).astype(jnp.bfloat16)
+    for columns in chunks:
+        next_query[:, columns] = (dot(normed, q_panel[:, columns]) * scale).astype(jnp.bfloat16)
 
 
 def last_kernel(
@@ -245,10 +246,10 @@
         )
         gathered = jnp.concatenate(
             [
+                jnp.where(core == 0, keep, beside),
+                jnp.where(core == 0, beside, keep),
                 jnp.where(core == 0, along, across),
                 jnp.where(core == 0, across, along),
-                jnp.where(core == 0, keep, beside),
-                jnp.where(core == 0, beside, keep),
             ],
             axis=0,
         )
@@ -264,15 +265,20 @@
         gathered, query, o_other = after(gathered, query, o_other)
 
         partial_shape = jax.ShapeDtypeStruct((2, count, width), jnp.float32)
-        first, second = pl.pallas_call(
-            latent_kernel,
-            out_shape=(partial_shape, partial_shape),
-            in_specs=[VMEM] * 3,
-            out_specs=(VMEM, VMEM),
-            compiler_params=params,
-            cost_estimate=cost(latent_cost),
-        )(gathered, k_weight, v_weight)
+        def partial_sums(layer, rows):
+            return pl.pallas_call(
+                functools.partial(latent_kernel, layer=layer),
+                out_shape=partial_shape,
+                in_specs=[VMEM] * 3,
+                out_specs=VMEM,
+                compiler_params=params,
+                cost_estimate=cost(latent_cost // 2),
+            )(rows, k_weight, v_weight)
+
+        first = partial_sums(0, gathered)
         first_other = swap(first)
+        _, gathered = after(first, gathered)
+        second = partial_sums(1, gathered)
         first_other, second = after(first_other, second)
         second_other = swap(second)
 

time: 29 us -> 28.7 us (0.990)
  waiting for transfers between devices: 6.67 us -> 6.22 us
    ppermute x4, waiting for transfers between devices: 2.65 us -> 2.19 us  [swap(): return lax.ppermute(array, 'narrow', [(0, 1), (1, 0)])]
    pallas_call x1 -> x2, Pallas kernels: 0.76 us -> 0.92 us  [partial_sums(): pl.pallas_call(functools.partial(latent_kernel, layer=layer), out_shape=p...]
  transfers between devices with their start and end apart: 9 -> 9, of which waited for: 4 -> 4; matrix products, arithmetic and copies ran while one was open for 0% -> 0% of each run, Pallas kernels for 27% -> 29%
where the time goes in v6:
time: 28.7 us; the launch traced here: 28.4 us
  Pallas kernels  12.7 us (44%)
  starting transfers between devices  8.59 us (30%)
  waiting for transfers between devices  6.22 us (22%)
  local copies, waits for them, and re-layouts  0.75 us (3%)
    ppermute x2, starting transfers between devices, shards(): lax.ppermute(source, 'wide', [(i, i ^ step) for i in range(wide)])  5.57 us
    pallas_call x1, Pallas kernels, shards(): pl.pallas_call(functools.partial(first_kernel, scale=scale, block=block),...  5.06 us
    pallas_call x1, Pallas kernels, shards(): pl.pallas_call(functools.partial(last_kernel, block=block, chunk=256), ou...  4.04 us
    ppermute x3, waiting for transfers between devices, shards(): lax.ppermute(array, ('wide', 'narrow'), [(i, i ^ mask) for i in devices])  2.42 us
    ppermute x3, starting transfers between devices, shards(): lax.ppermute(array, ('wide', 'narrow'), [(i, i ^ mask) for i in devices])  2.2 us
    ppermute x4, waiting for transfers between devices, swap(): return lax.ppermute(array, 'narrow', [(0, 1), (1, 0)])  2.19 us
    ppermute x2, waiting for transfers between devices, shards(): lax.ppermute(source, 'wide', [(i, i ^ step) for i in range(wide)])  1.61 us
    pallas_call x1, Pallas kernels, shards(): pl.pallas_call(norm_kernel, out_shape=(hidden_shape, jax.ShapeDtypeStruct...  1.38 us
  transfers between devices with their start and end apart: 9, of which 4 were waited for; matrix products, arithmetic and copies ran while one was open for 0% of the time, Pallas kernels for 29%

profile of v6, /device:TPU:0, one launch (start us, length us, event | category | flops | bytes accessed | tf_op | source)
XLA Modules:
  0.0 28.4 jit_solution(16099288238173970869)
XLA Ops:
  0.0 0.5 %collective-permute-start.2 = (bf16[2,512,1024]{2,1,0:T(8,128)(2,1)}, bf16[2,512,1024]{2,1,0:T(8,128)(2,1)}, u32[]{:S(2)}, u32[]{:S(2)}) collective-permute-start(bf16[2,512,1024]{2,1,0:T(8,128)(2,1)} %q_own.3), channel_id=1, source_target_pairs={{0,1},{1,0},{2,3},{3,2},{4,5},{5,4},{6,7},{7,6},{8,9},{9,8},{10,11... | collective-permute-start | bytes 6291464 | tf_op jit(solution)/shard_map/ppermute | solution.py:175
  0.5 3.7 %collective-permute-start = (bf16[8,1024]{1,0:T(8,128)(2,1)}, bf16[8,1024]{1,0:T(8,128)(2,1)S(1)}, u32[]{:S(2)}, u32[]{:S(2)}) collective-permute-start(bf16[8,1024]{1,0:T(8,128)(2,1)} %latents.1), channel_id=1, source_target_pairs={{0,8},{2,10},{4,12},{6,14},{8,0},{10,2},{12,4},{14,6},{1,9},{3,11}... | collective-permute-start | bytes 49160 | tf_op jit(solution)/shard_map/ppermute | solution.py:220
  4.1 0.2 collective-permute-start.6
  4.3 0.7 %copy-done.6 = bf16[8,1024]{1,0:T(8,128)(2,1)S(1)} copy-done((bf16[8,1024]{1,0:T(8,128)(2,1)S(1)}, bf16[8,1024]{1,0:T(8,128)(2,1)}, u32[]{:S(2)}) %copy-start.6) | copy-done | bytes 16408
  5.0 1.0 %collective-permute-done = bf16[8,1024]{1,0:T(8,128)(2,1)S(1)} collective-permute-done((bf16[8,1024]{1,0:T(8,128)(2,1)}, bf16[8,1024]{1,0:T(8,128)(2,1)S(1)}, u32[]{:S(2)}, u32[]{:S(2)}) %collective-permute-start) | collective-permute-done | bytes 16416 | tf_op jit(solution)/shard_map/ppermute | solution.py:220
  6.1 1.9 %collective-permute-start.1 = (bf16[16,1024]{1,0:T(8,128)(2,1)S(1)}, bf16[16,1024]{1,0:T(8,128)(2,1)S(1)}, u32[]{:S(2)}, u32[]{:S(2)}) collective-permute-start(bf16[16,1024]{1,0:T(8,128)(2,1)S(1)} %pad_maximum_fusion.1), channel_id=1, source_target_pairs={{0,4},{2,6},{4,0},{6,2},{8,12},{10,14},{12,8},{14,10},{1,5},{3,7},... | collective-permute-start | bytes 98312 | tf_op jit(solution)/shard_map/ppermute | solution.py:220
  8.0 0.0 collective-permute-done.2.q_other
  8.0 1.4 %shard_map.74 = (bf16[512,1024]{1,0:T(8,128)(2,1)S(1)}, bf16[512,1024]{1,0:T(8,128)(2,1)S(1)}) custom-call(bf16[512,1024]{1,0:T(8,128)(2,1)S(1)} %copy-done.4, f32[2,1024]{1,0:T(2,128)S(1)} %copy-done.5, bf16[2,512,1024]{2,1,0:T(8,128)(2,1)} %collective-permute-done.2.q_other), custom_call_target="tpu_custom_call" | custom-call | flops 4294967296 | bytes 4194304 | tf_op jit(solution)/shard_map/pallas_call | solution.py:223
  9.4 0.6 %collective-permute-done.1 = bf16[16,1024]{1,0:T(8,128)(2,1)S(1)} collective-permute-done((bf16[16,1024]{1,0:T(8,128)(2,1)S(1)}, bf16[16,1024]{1,0:T(8,128)(2,1)S(1)}, u32[]{:S(2)}, u32[]{:S(2)}) %collective-permute-start.1) | collective-permute-done | bytes 32800 | tf_op jit(solution)/shard_map/ppermute | solution.py:220
  10.0 0.1 collective-permute-start.5
  10.1 1.9 %collective-permute-start.3 = (bf16[32,512]{1,0:T(8,128)(2,1)S(1)}, bf16[32,512]{1,0:T(8,128)(2,1)S(1)}, u32[]{:S(2)}, u32[]{:S(2)}) collective-permute-start(bf16[32,512]{1,0:T(8,128)(2,1)S(1)} %get-tuple-element.27), channel_id=1, source_target_pairs={{0,1},{1,0},{2,3},{3,2},{4,5},{5,4},{6,7},{7,6},{8,9},{9,8},{10,11... | collective-permute-start | bytes 98312 | tf_op jit(solution)/shard_map/ppermute | solution.py:244
  12.0 0.2 collective-permute-start.4
  12.2 1.3 %shard_map.75.query = bf16[512,1024]{1,0:T(8,128)(2,1)S(1)} custom-call(s32[1]{0:T(128)} %bitcast.narrow, bf16[512,1024]{1,0:T(8,128)(2,1)S(1)} %get-tuple-element.28.normed, bf16[2,512,1024]{2,1,0:T(8,128)(2,1)S(1)} %copy-done.1, bf16[512,1024]{1,0:T(8,128)(2,1)S(1)} %get-tuple-element.29.q_other), custom_call_target="tpu_custom_call" | custom-call | flops 1073741824 | bytes 4194304 | tf_op jit(solution)/shard_map/pallas_call | solution.py:257
  13.5 2.4 %collective-permute-done.4 = bf16[32,512]{1,0:T(8,128)(2,1)S(1)} collective-permute-done((bf16[32,512]{1,0:T(8,128)(2,1)S(1)}, bf16[32,512]{1,0:T(8,128)(2,1)S(1)}, u32[]{:S(2)}, u32[]{:S(2)}) %collective-permute-start.4) | collective-permute-done | bytes 32800 | tf_op jit(solution)/shard_map/ppermute | solution.py:244
  15.9 0.0 collective-permute-done.5
  15.9 0.0 collective-permute-done.6.o_other
  16.0 0.5 %shard_map.76.mine = f32[2,128,1024]{2,1,0:T(8,128)S(1)} custom-call(bf16[128,512]{1,0:T(8,128)(2,1)S(1)} %pad_maximum_fusion.latents, bf16[2,512,1024]{2,1,0:T(8,128)(2,1)S(1)} %copy-done.2, bf16[2,512,1024]{2,1,0:T(8,128)(2,1)S(1)} %copy-done.3), custom_call_target="tpu_custom_call" | custom-call | flops 268435456 | bytes 4194304 | tf_op jit(solution)/shard_map/pallas_call | solution.py:269
  16.4 0.0 copy-start
  16.4 0.1 collective-permute-start.7
  16.5 0.5 %shard_map.77.mine = f32[2,128,1024]{2,1,0:T(8,128)S(1)} custom-call(bf16[128,512]{1,0:T(8,128)(2,1)S(1)} %pad_maximum_fusion.latents, bf16[2,512,1024]{2,1,0:T(8,128)(2,1)S(1)} %copy-done.2, bf16[2,512,1024]{2,1,0:T(8,128)(2,1)S(1)} %copy-done.3), custom_call_target="tpu_custom_call" | custom-call | flops 268435456 | bytes 4194304 | tf_op jit(solution)/shard_map/pallas_call | solution.py:269
  17.0 2.2 %collective-permute-done.7.theirs = f32[2,128,1024]{2,1,0:T(8,128)S(1)} collective-permute-done((f32[2,128,1024]{2,1,0:T(8,128)S(1)}, f32[2,128,1024]{2,1,0:T(8,128)S(1)}, u32[]{:S(2)}, u32[]{:S(2)}) %collective-permute-start.7) | collective-permute-done | bytes 1048608 | tf_op jit(solution)/shard_map/ppermute | solution.py:175
  19.2 0.1 collective-permute-start.8
  19.3 5.1 %shard_map.78 = (bf16[512,1024]{1,0:T(8,128)(2,1)S(1)}, bf16[512,1024]{1,0:T(8,128)(2,1)S(1)}) custom-call(s32[1]{0:T(128)} %bitcast.narrow, bf16[512,1024]{1,0:T(8,128)(2,1)S(1)} %copy-done.4, bf16[512,1024]{1,0:T(8,128)(2,1)S(1)} %shard_map.75.query, bf16[256,128]{1,0:T(8,128)(2,1)S(1)} %get-tuple-element.31.ones, f32[2,128,1024]{2,1,0:T(8,128)S(1)} %shard_map.76.mine, ...), custom_call_target="tpu_custom_call" | custom-call | flops 2684354560 | bytes 4194304 | tf_op jit(solution)/shard_map/pallas_call | solution.py:285
  24.4 4.0 %shard_map.79 = bf16[512,1024]{1,0:T(8,128)(2,1)} custom-call(s32[1]{0:T(128)} %bitcast.narrow, bf16[512,1024]{1,0:T(8,128)(2,1)S(1)} %get-tuple-element.36.hidden, bf16[512,1024]{1,0:T(8,128)(2,1)S(1)} %get-tuple-element.37.query, bf16[256,128]{1,0:T(8,128)(2,1)S(1)} %get-tuple-element.31.ones, f32[2,128,1024]{2,1,0:T(8,128)S(1)} %shard_map.77.mine, ...), custom_call_target="tpu_custom_call" | custom-call | flops 1610612736 | bytes 4194304 | tf_op jit(solution)/shard_map/pallas_call | solution.py:294
  (23 shorter events, 0.1 us)
Async XLA Ops:
  0.0 8.0 %copy-start.5 = (f32[2,1024]{1,0:T(2,128)S(1)}, f32[2,1024]{1,0:T(2,128)}, u32[]{:S(2)}) copy-start(f32[2,1024]{1,0:T(2,128)} %gains.3) | copy-start | bytes 24580
  0.0 8.0 %copy-start.4 = (bf16[512,1024]{1,0:T(8,128)(2,1)S(1)}, bf16[512,1024]{1,0:T(8,128)(2,1)}, u32[]{:S(2)}) copy-start(bf16[512,1024]{1,0:T(8,128)(2,1)} %hidden.3) | copy-start | bytes 3145732
  0.0 8.0 %collective-permute-start.2 = (bf16[2,512,1024]{2,1,0:T(8,128)(2,1)}, bf16[2,512,1024]{2,1,0:T(8,128)(2,1)}, u32[]{:S(2)}, u32[]{:S(2)}) collective-permute-start(bf16[2,512,1024]{2,1,0:T(8,128)(2,1)} %q_own.3), channel_id=1, source_target_pairs={{0,1},{1,0},{2,3},{3,2},{4,5},{5,4},{6,7},{7,6},{8,9},{9,8},{10,11... | collective-permute-start | bytes 6291464 | tf_op jit(solution)/shard_map/ppermute | solution.py:175
  0.5 5.6 %collective-permute-start = (bf16[8,1024]{1,0:T(8,128)(2,1)}, bf16[8,1024]{1,0:T(8,128)(2,1)S(1)}, u32[]{:S(2)}, u32[]{:S(2)}) collective-permute-start(bf16[8,1024]{1,0:T(8,128)(2,1)} %latents.1), channel_id=1, source_target_pairs={{0,8},{2,10},{4,12},{6,14},{8,0},{10,2},{12,4},{14,6},{1,9},{3,11}... | collective-permute-start | bytes 49160 | tf_op jit(solution)/shard_map/ppermute | solution.py:220
  4.1 11.8 %collective-permute-start.6 = (bf16[2,512,1024]{2,1,0:T(8,128)(2,1)}, bf16[2,512,1024]{2,1,0:T(8,128)(2,1)S(1)}, u32[]{:S(2)}, u32[]{:S(2)}) collective-permute-start(bf16[2,512,1024]{2,1,0:T(8,128)(2,1)} %o_own.3), channel_id=1, source_target_pairs={{0,1},{1,0},{2,3},{3,2},{4,5},{5,4},{6,7},{7,6},{8,9},{9,8},{10,11... | collective-permute-start | bytes 6291464 | tf_op jit(solution)/shard_map/ppermute | solution.py:175
  4.3 0.7 %copy-start.6 = (bf16[8,1024]{1,0:T(8,128)(2,1)S(1)}, bf16[8,1024]{1,0:T(8,128)(2,1)}, u32[]{:S(2)}) copy-start(bf16[8,1024]{1,0:T(8,128)(2,1)} %latents.1) | copy-start | bytes 49156
  6.1 3.9 %collective-permute-start.1 = (bf16[16,1024]{1,0:T(8,128)(2,1)S(1)}, bf16[16,1024]{1,0:T(8,128)(2,1)S(1)}, u32[]{:S(2)}, u32[]{:S(2)}) collective-permute-start(bf16[16,1024]{1,0:T(8,128)(2,1)S(1)} %pad_maximum_fusion.1), channel_id=1, source_target_pairs={{0,4},{2,6},{4,0},{6,2},{8,12},{10,14},{12,8},{14,10},{1,5},{3,7},... | collective-permute-start | bytes 98312 | tf_op jit(solution)/shard_map/ppermute | solution.py:220
  8.0 4.2 %copy-start.1 = (bf16[2,512,1024]{2,1,0:T(8,128)(2,1)S(1)}, bf16[2,512,1024]{2,1,0:T(8,128)(2,1)}, u32[]{:S(2)}) copy-start(bf16[2,512,1024]{2,1,0:T(8,128)(2,1)} %q_own.3) | copy-start | bytes 6291460
  10.0 5.9 %collective-permute-start.5 = (bf16[32,512]{1,0:T(8,128)(2,1)S(1)}, bf16[32,512]{1,0:T(8,128)(2,1)S(1)}, u32[]{:S(2)}, u32[]{:S(2)}) collective-permute-start(bf16[32,512]{1,0:T(8,128)(2,1)S(1)} %get-tuple-element.27), channel_id=1, source_target_pairs={{0,3},{1,2},{2,1},{3,0},{4,7},{5,6},{6,5},{7,4},{8,11},{9,10},{10,... | collective-permute-start | bytes 98312 | tf_op jit(solution)/shard_map/ppermute | solution.py:244
  10.1 3.4 %collective-permute-start.3 = (bf16[32,512]{1,0:T(8,128)(2,1)S(1)}, bf16[32,512]{1,0:T(8,128)(2,1)S(1)}, u32[]{:S(2)}, u32[]{:S(2)}) collective-permute-start(bf16[32,512]{1,0:T(8,128)(2,1)S(1)} %get-tuple-element.27), channel_id=1, source_target_pairs={{0,1},{1,0},{2,3},{3,2},{4,5},{5,4},{6,7},{7,6},{8,9},{9,8},{10,11... | collective-permute-start | bytes 98312 | tf_op jit(solution)/shard_map/ppermute | solution.py:244
  12.0 3.9 %collective-permute-start.4 = (bf16[32,512]{1,0:T(8,128)(2,1)S(1)}, bf16[32,512]{1,0:T(8,128)(2,1)S(1)}, u32[]{:S(2)}, u32[]{:S(2)}) collective-permute-start(bf16[32,512]{1,0:T(8,128)(2,1)S(1)} %get-tuple-element.26), channel_id=1, source_target_pairs={{0,2},{1,3},{2,0},{3,1},{4,6},{5,7},{6,4},{7,5},{8,10},{9,11},{10,... | collective-permute-start | bytes 98312 | tf_op jit(solution)/shard_map/ppermute | solution.py:244
  12.2 3.8 %copy-start.2 = (bf16[2,512,1024]{2,1,0:T(8,128)(2,1)S(1)}, bf16[2,512,1024]{2,1,0:T(8,128)(2,1)}, u32[]{:S(2)}) copy-start(bf16[2,512,1024]{2,1,0:T(8,128)(2,1)} %k_own.3) | copy-start | bytes 6291460
  12.2 3.8 %copy-start.3 = (bf16[2,512,1024]{2,1,0:T(8,128)(2,1)S(1)}, bf16[2,512,1024]{2,1,0:T(8,128)(2,1)}, u32[]{:S(2)}) copy-start(bf16[2,512,1024]{2,1,0:T(8,128)(2,1)} %v_own.3) | copy-start | bytes 6291460
  16.4 2.9 %copy-start = (bf16[2,512,1024]{2,1,0:T(8,128)(2,1)S(1)}, bf16[2,512,1024]{2,1,0:T(8,128)(2,1)}, u32[]{:S(2)}) copy-start(bf16[2,512,1024]{2,1,0:T(8,128)(2,1)} %o_own.3) | copy-start | bytes 6291460
  16.4 2.7 %collective-permute-start.7 = (f32[2,128,1024]{2,1,0:T(8,128)S(1)}, f32[2,128,1024]{2,1,0:T(8,128)S(1)}, u32[]{:S(2)}, u32[]{:S(2)}) collective-permute-start(f32[2,128,1024]{2,1,0:T(8,128)S(1)} %shard_map.76.mine), channel_id=1, source_target_pairs={{0,1},{1,0},{2,3},{3,2},{4,5},{5,4},{6,7},{7,6},{8,9},{9,8},{10,11... | collective-permute-start | bytes 3145736 | tf_op jit(solution)/shard_map/ppermute | solution.py:175
  19.2 5.2 %collective-permute-start.8 = (f32[2,128,1024]{2,1,0:T(8,128)S(1)}, f32[2,128,1024]{2,1,0:T(8,128)S(1)}, u32[]{:S(2)}, u32[]{:S(2)}) collective-permute-start(f32[2,128,1024]{2,1,0:T(8,128)S(1)} %shard_map.77.mine), channel_id=1, source_target_pairs={{0,1},{1,0},{2,3},{3,2},{4,5},{5,4},{6,7},{7,6},{8,9},{9,8},{10,11... | collective-permute-start | bytes 3145736 | tf_op jit(solution)/shard_map/ppermute | solution.py:175
